TPU v7x, 128 devices: a whole 4x4x4 slice. The times are simulated.
128 devices in a mesh: task: 4 (over x), patch: 32 (over z, y, core).
Axes of the slice: x: 4, y: 4, z: 4, core: 2. Of those that a mesh axis runs over, the one named last changes fastest.
Arguments:
- trials_initial_dye: float32 [64, 4, 256, 1024], P('task', None, 'patch'), may hold values from -6 to 6
- diffusivity: float32 [4], replicated, may hold values from 0.02 to 0.2
- wet_mask: int32 [256, 1024], P('patch'), may hold values 0 or 1
- deeper_donor_tier: int32 [4, 256, 1024], P(None, 'patch'), may hold values from 0 to 2
- shallower_tier_fraction: float32 [4, 256, 1024], P(None, 'patch'), may hold values from 0 to 1
- obs_pos: int32 [262144], P('patch'), may hold values from 0 to 8191, as said below
- obs_value: float32 [262144], P('patch'), may hold values from -6 to 6
- obs_var: float32 [262144], P('patch'), may hold values from 0.5 to 2
- observation_list: int32 [64, 256, 32], P('patch', 'task'), may hold values from 0 to 262143, as said below
- obs_count: int32 [64, 256], P('patch', 'task'), may hold values from 1 to 32, as said below
Outputs:
- analysis: float32 [64, 4, 256, 1024], P('task', None, 'patch')
Inputs may be any that keep to these rules, and one draw needn't show every extreme that they name: `obs_pos`: observation k of strip s (entry s * 8192 + k) lies in column k // 8 of the strip; the entry is its row within the strip times 1024 plus that column. `observation_list`: each listed observation lies in a strip at most two strips from the coarse point's strip and in a column at most 4 columns from the point's block's first column; entries may repeat. `obs_count`: slots at and beyond the count are ignored.
All inputs are finite; a program needn't handle non-finite values. No bound on the sum of `wet_mask` on one device may be relied on, other than what follows from the above.
Results may differ from a plain program's by a relative error of at most 0.0003.
Values sent between devices are 32-bit elements; how exact they have to be, the bound alone decides.
A program may use at most 384 MiB of HBM per device.

v0:
```python
import jax
import jax.numpy as jnp
from jax import lax
from jax.sharding import PartitionSpec as P

LEV = 4
STEPS = 4
COARSE = 4
LOC = 24
NS_ITERS = 6


def padded_2(cells, sides, width):
    for axis, dim in sides:
        count = lax.axis_size(axis)
        ends = count - 1
        head = lax.slice_in_dim(cells, 0, width, axis=dim)
        tail = lax.slice_in_dim(cells, cells.shape[dim] - width, cells.shape[dim], axis=dim)
        cells = jnp.concatenate(
            [
                lax.ppermute(tail, axis, [(i, (i + 1) % count) for i in range(ends)]),
                cells,
                lax.ppermute(head, axis, [((i + 1) % count, i) for i in range(ends)]),
            ],
            axis=dim,
        )
    return cells


def from_behind(x, axis, by):
    count = lax.axis_size(axis)
    pairs = [(i, i + by) for i in range(count) if 0 <= i + by < count]
    return lax.ppermute(x, axis, pairs)


def depthwise_regridding(dye_map, deeper_donor_tier, shallower_tier_fraction):
    lower_value = jnp.zeros_like(dye_map)
    upper_value = jnp.zeros_like(dye_map)
    for level_no in range(LEV - 1):
        chosen = deeper_donor_tier == level_no
        lower_value = jnp.where(chosen, dye_map[..., level_no : level_no + 1, :, :], lower_value)
        upper_value = jnp.where(
            chosen, dye_map[..., level_no + 1 : level_no + 2, :, :], upper_value
        )
    return (1.0 - shallower_tier_fraction) * lower_value + shallower_tier_fraction * upper_value


def point_weights(ens_obs, innovation, obs_var, obs_row, obs_col, point_row, point_col, live_slot):
    trial_tally = ens_obs.shape[0]
    dist_sq = (obs_row - point_row) ** 2 + (obs_col - point_col) ** 2
    taper_weight = jnp.where(live_slot, jnp.exp(-dist_sq / (2.0 * LOC * LOC)) / obs_var, 0.0)
    scaled = ens_obs * taper_weight
    gram_matrix = jnp.einsum("ikp,jkp->ijp", scaled, ens_obs, precision=lax.Precision.HIGHEST)
    identity_mat = jnp.eye(trial_tally, dtype=jnp.float32)[:, :, None]
    system = (trial_tally - 1.0) * identity_mat + gram_matrix
    frobenius = jnp.sqrt(jnp.sum(system * system, axis=(0, 1)))
    root_iter = system / frobenius
    inverse_root = jnp.broadcast_to(identity_mat, system.shape)
    for turn_no in range(NS_ITERS):
        middle = 1.5 * identity_mat - 0.5 * jnp.einsum(
            "ijp,jkp->ikp", inverse_root, root_iter, precision=lax.Precision.HIGHEST
        )
        root_iter = jnp.einsum("ijp,jkp->ikp", root_iter, middle, precision=lax.Precision.HIGHEST)
        inverse_root = jnp.einsum(
            "ijp,jkp->ikp", middle, inverse_root, precision=lax.Precision.HIGHEST
        )
    drive_vec = jnp.einsum("ikp,kp->ip", scaled, innovation, precision=lax.Precision.HIGHEST)
    half_way = jnp.einsum("ijp,jp->ip", inverse_root, drive_vec, precision=lax.Precision.HIGHEST)
    mean_weight = (
        jnp.einsum("ijp,jp->ip", inverse_root, half_way, precision=lax.Precision.HIGHEST)
        / frobenius
    )
    return (
        jnp.sqrt(trial_tally - 1.0) / jnp.sqrt(frobenius) * inverse_root + mean_weight[:, None, :]
    )


def blend_weights(departure_rows, padded_weights):
    trial_tally, levels, coarse_rows, span_cells, width_cells = departure_rows.shape
    coarse_cols = padded_weights.shape[3] - 2
    offset = (jnp.arange(span_cells, dtype=jnp.float32) - 0.5 * (span_cells - 1)) / span_cells
    coefficients = [jnp.maximum(-offset, 0.0), 1.0 - jnp.abs(offset), jnp.maximum(offset, 0.0)]
    blended = jnp.zeros_like(departure_rows)
    for row_shift in range(3):
        row_weights = padded_weights[:, :, row_shift : row_shift + coarse_rows]
        column_weights = jnp.zeros(
            (trial_tally, trial_tally, coarse_rows, coarse_cols, span_cells), jnp.float32
        )
        for col_shift in range(3):
            column_weights = (
                column_weights
                + row_weights[..., col_shift : col_shift + coarse_cols, None]
                * coefficients[col_shift]
            )
        column_weights = column_weights.reshape(trial_tally, trial_tally, coarse_rows, width_cells)
        product_term = jnp.einsum(
            "ilarx,ijax->jlarx", departure_rows, column_weights, precision=lax.Precision.HIGHEST
        )
        blended = blended + coefficients[row_shift][:, None] * product_term
    return blended - departure_rows


def body(
    trials_initial_dye,
    diffusivity,
    wet_mask,
    deeper_donor_tier,
    shallower_tier_fraction,
    obs_pos,
    obs_value,
    obs_var,
    observation_list,
    obs_count,
):
    batch_span, levels, northings_each_zone, easting_sequence = trials_initial_dye.shape
    strip_index = lax.axis_index("patch")
    column_block = lax.axis_index("task")
    strips = lax.axis_size("patch")
    column_blocks = lax.axis_size("task")
    ocean = wet_mask.astype(jnp.float32)
    diffusion_rate = diffusivity[None, :, None, None]
    dye_map = trials_initial_dye
    for time_step in range(STEPS):
        rimmed = padded_2(dye_map, (("patch", 2),), 1)
        padded = jnp.pad(rimmed, ((0, 0), (0, 0), (0, 0), (1, 1)))
        beside_all = (
            padded[:, :, 2:, 1:-1]
            + padded[:, :, :-2, 1:-1]
            + padded[:, :, 1:-1, 2:]
            + padded[:, :, 1:-1, :-2]
        )
        dye_map = ocean * (dye_map + diffusion_rate * (beside_all - 4.0 * dye_map))
    propagated_condition = depthwise_regridding(dye_map, deeper_donor_tier, shallower_tier_fraction)
    observation_slots = obs_pos.shape[0]
    seaface_map = propagated_condition[:, 0].reshape(
        batch_span, northings_each_zone * easting_sequence
    )
    own_obs = jnp.take(seaface_map, obs_pos, axis=1)
    obs_row = (strip_index * northings_each_zone + obs_pos // easting_sequence).astype(jnp.float32)
    obs_col = (obs_pos % easting_sequence).astype(jnp.float32)
    obs_pack = jnp.stack([obs_value, obs_var, obs_row, obs_col])
    reaches = (2, 1, -1, -2)
    first_piece_index = 0
    copies = jnp.tile(own_obs[:, None, None, :], (1, 1, 1, column_blocks))
    ensemble, gathered = (
        lax.all_to_all(propagated_condition, "task", split_axis=3, concat_axis=0, tiled=True),
        lax.all_to_all(copies, "task", split_axis=3, concat_axis=0, tiled=True),
    )
    trial_tally = ensemble.shape[0]
    quarter = ensemble.shape[3]
    carried_all = gathered.reshape(trial_tally, -1)
    moved_pieces = [from_behind((carried_all, obs_pack), "patch", reach) for reach in reaches]
    window_obs = jnp.concatenate(
        [
            moved_pieces[0][0],
            moved_pieces[1][0],
            carried_all,
            moved_pieces[2][0],
            moved_pieces[3][0],
        ],
        axis=1,
    )
    window_pack = jnp.concatenate(
        [moved_pieces[0][1], moved_pieces[1][1], obs_pack, moved_pieces[2][1], moved_pieces[3][1]],
        axis=1,
    )
    sample_centroid = jnp.mean(ensemble, axis=0)
    trial_departure = ensemble - sample_centroid
    obs_mean = jnp.mean(window_obs, axis=0)
    obs_pert = window_obs - obs_mean
    innovation = window_pack[0] - obs_mean
    reduced_northing_tally, reduced_easting_tally, berth_tally = observation_list.shape
    strip_start_row = observation_list // observation_slots - (strip_index - 2)
    relocated_ordinal = (
        strip_start_row * observation_slots
        + observation_list % observation_slots
        - first_piece_index
    )
    sensor_ordinal = relocated_ordinal.reshape(
        reduced_northing_tally * reduced_easting_tally, berth_tally
    ).T
    live_slot = jnp.arange(berth_tally)[:, None] < obs_count.reshape(-1)[None, :]
    half_cell = 0.5 * (COARSE - 1)
    row_values = (
        strip_index * northings_each_zone + COARSE * jnp.arange(reduced_northing_tally)
    ).astype(jnp.float32) + half_cell
    col_values = (column_block * quarter + COARSE * jnp.arange(reduced_easting_tally)).astype(
        jnp.float32
    ) + half_cell
    point_row = jnp.broadcast_to(
        row_values[:, None], (reduced_northing_tally, reduced_easting_tally)
    ).reshape(-1)
    point_col = jnp.broadcast_to(
        col_values[None, :], (reduced_northing_tally, reduced_easting_tally)
    ).reshape(-1)
    weights = point_weights(
        jnp.take(obs_pert, sensor_ordinal, axis=1),
        jnp.take(innovation, sensor_ordinal),
        jnp.take(window_pack[1], sensor_ordinal),
        jnp.take(window_pack[2], sensor_ordinal),
        jnp.take(window_pack[3], sensor_ordinal),
        point_row,
        point_col,
        live_slot,
    )
    coarse_tiles = weights.reshape(
        trial_tally, trial_tally, reduced_northing_tally, reduced_easting_tally
    )
    extended = padded_2(coarse_tiles, (("task", 3), ("patch", 2)), 1)
    top_row = jnp.where(strip_index == 0, extended[:, :, 1:2], extended[:, :, 0:1])
    bottom_row = jnp.where(strip_index == strips - 1, extended[:, :, -2:-1], extended[:, :, -1:])
    extended = jnp.concatenate([top_row, extended[:, :, 1:-1], bottom_row], axis=2)
    left_col = jnp.where(column_block == 0, extended[..., 1:2], extended[..., 0:1])
    right_col = jnp.where(
        column_block == column_blocks - 1, extended[..., -2:-1], extended[..., -1:]
    )
    extended = jnp.concatenate([left_col, extended[..., 1:-1], right_col], axis=3)
    departure_rows = trial_departure.reshape(
        trial_tally, levels, reduced_northing_tally, COARSE, quarter
    )
    ocean_here = lax.dynamic_slice_in_dim(ocean, column_block * quarter, quarter, 1)
    kalman_adjustment = (
        blend_weights(departure_rows, extended).reshape(
            trial_tally, levels, northings_each_zone, quarter
        )
        * ocean_here
    )
    delivered_portions = lax.all_to_all(
        kalman_adjustment, "task", split_axis=0, concat_axis=3, tiled=True
    )
    return propagated_condition + delivered_portions


def solution(mesh):
    return jax.shard_map(
        body,
        mesh=mesh,
        in_specs=(
            P("task", None, "patch", None),
            P(),
            P("patch", None),
            P(None, "patch", None),
            P(None, "patch", None),
            P("patch"),
            P("patch"),
            P("patch"),
            P("patch", "task", None),
            P("patch", "task"),
        ),
        out_specs=P("task", None, "patch", None),
        check_vma=False,
    )
```

profile of v0, /device:TPU:0, one launch (start us, length us, event | category | flops | bytes accessed | tf_op | source)
XLA Modules:
  0.0 1127.9 jit_solution(9348562549591089409)
XLA Ops:
  62.0 30.1 %gather_fusion = f32[8192,16]{1,0:T(8,128)} fusion(f32[16,8192]{0,1:T(8,128)} %bitcast.267, s32[8192]{0:T(1024)S(1)} %get-tuple-element.49), kind=kCustom, calls=%fused_computation.4 | custom fusion | bytes 1081344 | tf_op jit(solution)/shard_map/jit(_take)/gather | solution.py:138
  105.8 146.5 %reduce.1 = f32[32768,16]{1,0:T(8,128)} reduce(f32[32768,1,1,16]{3,2,1,0:T(1,128)} %bitcast.260, f32[]{:T(128)} %broadcast.469), dimensions={1,2}, to_apply=%bitcast.236.reduce_sub_computation | reduce | bytes 4194308
  252.3 10.1 reshape.262
  269.4 21.7 %all-to-all-done = f32[4,1,131072]{2,1,0:T(1,128)} async-done(((f32[4,1,131072]{2,1,0:T(1,128)}), f32[4,1,131072]{2,1,0:T(1,128)}, u32[]{:S(2)}, u32[]{:S(2)}) %all-to-all-start) | async-done | bytes 2097184 | tf_op jit(solution)/shard_map/all_to_all | solution.py:147
  300.1 45.6 %reshape.263 = f32[32768,1,1,16]{3,2,1,0:T(1,128)} reshape(f32[4,131072]{1,0:T(4,128)} %reduce.2) | data formatting | bytes 4194304
  345.8 11.0 copy.272
  360.9 13.0 %collective-permute-start.8 = (f32[64,8192]{1,0:T(8,128)}, f32[64,8192]{1,0:T(8,128)}, u32[]{:S(2)}, u32[]{:S(2)}) collective-permute-start(f32[64,8192]{1,0:T(8,128)} %bitcast.10), channel_id=1, source_target_pairs={{0,2},{1,3},{2,4},{3,5},{4,6},{5,7},{6,8},{7,9},{8,10},{9,11},{10,... | collective-permute-start | bytes 6291464 | tf_op jit(solution)/shard_map/ppermute | solution.py:33
  378.2 23.0 %gather_fusion.4 = f32[4096]{0:T(1024)S(1)} fusion(f32[40960]{0:T(1024)S(1)} %bitcast.250, s32[4096]{0:T(1024)S(1)} %bitcast_clamp_fusion), kind=kCustom, calls=%fused_computation.2.clone | custom fusion | bytes 49152 | tf_op jit(solution)/shard_map/jit(_take)/gather | solution.py:199
  401.3 23.0 %gather_fusion.3 = f32[4096]{0:T(1024)S(1)} fusion(f32[40960]{0:T(1024)S(1)} %bitcast.249, s32[4096]{0:T(1024)S(1)} %bitcast_clamp_fusion), kind=kCustom, calls=%fused_computation.1.clone | custom fusion | bytes 49152 | tf_op jit(solution)/shard_map/jit(_take)/gather | solution.py:201
  424.3 23.0 %gather_fusion.2 = f32[4096]{0:T(1024)S(1)} fusion(f32[40960]{0:T(1024)S(1)} %bitcast.248, s32[4096]{0:T(1024)S(1)} %bitcast_clamp_fusion), kind=kCustom, calls=%fused_computation.clone | custom fusion | bytes 49152 | tf_op jit(solution)/shard_map/jit(_take)/gather | solution.py:200
  447.4 13.6 %copy.231 = f32[16,4,8,1024]{0,2,1,3:T(8,128)} copy(f32[16,4,8,1024]{3,2,1,0:T(8,128)S(1)} %multiply_add_fusion) | data formatting | bytes 4194304 | tf_op jit(solution)/shard_map/add | solution.py:45
  461.0 10.1 reshape.264
  506.1 23.7 %collective-permute-done.11 = f32[64,8192]{1,0:T(8,128)S(1)} collective-permute-done((f32[64,8192]{1,0:T(8,128)}, f32[64,8192]{1,0:T(8,128)S(1)}, u32[]{:S(2)}, u32[]{:S(2)}) %collective-permute-start.11) | collective-permute-done | bytes 2097184 | tf_op jit(solution)/shard_map/ppermute | solution.py:33
  537.1 10.1 reduce_sum.27
  547.3 15.5 %broadcast_subtract_fusion = f32[64,40960]{0,1:T(8,128)} fusion(f32[64,40960]{0,1:T(8,128)} %constant_dynamic-update-slice_fusion, f32[40960]{0:T(1024)S(1)} %get-tuple-element.44), kind=kLoop, calls=%fused_computation.27 | loop fusion | flops 2621440 | bytes 21135360 | tf_op jit(solution)/shard_map/sub | solution.py:170
  562.8 17.7 %gather_fusion.1 = f32[4096,64]{1,0:T(8,128)S(1)} fusion(f32[64,40960]{0,1:T(8,128)} %broadcast_subtract_fusion, s32[4096]{0:T(1024)S(1)} %bitcast_clamp_fusion), kind=kCustom, calls=%fused_computation.5 | custom fusion | bytes 2113536 | tf_op jit(solution)/shard_map/jit(_take)/gather | solution.py:197
  580.5 23.2 %gather_fusion.5 = f32[4096]{0:T(1024)S(1)} fusion(f32[40960]{0:T(1024)S(1)} %get-tuple-element.43, s32[4096]{0:T(1024)S(1)} %bitcast_clamp_fusion), kind=kCustom, calls=%fused_computation.3.clone | custom fusion | bytes 49152 | tf_op jit(solution)/shard_map/jit(_take)/gather | solution.py:198
  604.0 9.9 multiply_reduce_fusion
  772.6 11.6 %reshape.265 = f32[1024,4,8,16]{3,2,1,0:T(8,128)} reshape(f32[4,131072]{1,0:T(4,128)S(1)} %reduce.3) | data formatting | bytes 4194304
  784.2 10.7 copy.273
  828.7 21.5 %slice_select_fusion.1 = (f32[64,64,4,1]{3,1,2,0:T(8,128)}, f32[64,64,4,1]{3,1,2,0:T(8,128)}) fusion(f32[64,64,4,66]{3,1,2,0:T(8,128)} %copy-done, pred[]{:T(512)S(6)} %eq.69, pred[]{:T(512)S(6)} %eq.73), kind=kLoop, calls=%fused_computation.29 | loop fusion | flops 32768 | bytes 393218 | tf_op jit(solution)/shard_map/jit(_where)/select_n | solution.py:213
  850.2 25.7 %fusion.33 = (f32[64,64,2,64]{3,1,2,0:T(8,128)}, f32[64,64,2,64]{3,1,2,0:T(8,128)}, f32[64,64,2,64]{3,1,2,0:T(8,128)}, f32[64,64,2,64]{3,1,2,0:T(8,128)}, f32[64...) fusion(f32[64,64,4,1]{3,1,2,0:T(8,128)} %get-tuple-element.19, f32[64,64,4,64]{3,1,2,0:T(8,128)} %slice.291, ...), kind=kLoop, calls=%fused_computation.53 | loop fusion | flops 3145728 | bytes 16908288 | tf_op jit(solution)/shard_map/concatenate | solution.py:217
  919.3 10.6 mul.489
  938.0 10.4 mul.483
  948.5 26.8 %fusion = f32[2,256,64,4,4]{2,4,3,1,0:T(4,128)} fusion(f32[64,64,2,256]{1,0,3,2:T(8,128)} %bitcast.254, f32[64,64,2,256]{1,0,3,2:T(8,128)} %bitcast.256, f32[64,64,2,256]{1,0,3,2:T(8,128)} %bitcast.258, f32[256]{0:T(256)S(1)} %mul.467, f32[256]{0:T(256)S(1)} %mul.461, f32[256]{0:T(256)S(1)} %mul.455, f32[64,4,2,4,256]{0,3,1,4,2:T(4,128)} %copy.236, ...), kind=kOutput, calls=%fused_computation.6 | convolution fusion | flops 413663232 | bytes 29395968 | tf_op jit(solution)/shard_map/ilarx,ijax->jlarx/dot_general | solution.py:96
  975.3 10.6 mul.478
  994.0 10.4 mul.472
  1004.4 26.8 %fusion.2 = f32[2,256,64,4,4]{2,4,3,1,0:T(4,128)} fusion(f32[64,64,2,256]{1,0,3,2:T(8,128)} %bitcast.255, f32[64,64,2,256]{1,0,3,2:T(8,128)} %bitcast.257, f32[64,64,2,256]{1,0,3,2:T(8,128)} %bitcast.259, f32[256]{0:T(256)S(1)} %mul.467, f32[256]{0:T(256)S(1)} %mul.461, f32[256]{0:T(256)S(1)} %mul.455, f32[64,4,2,4,256]{0,3,1,4,2:T(4,128)} %copy.236, ...), kind=kOutput, calls=%fused_computation.8 | convolution fusion | flops 413663232 | bytes 29395968 | tf_op jit(solution)/shard_map/ilarx,ijax->jlarx/dot_general | solution.py:96
  1031.2 10.6 mul.464
  1049.9 10.6 mul.452
  1060.5 27.6 %bitcast_subtract_fusion = f32[64,4,2,4,256]{0,3,1,4,2:T(4,128)} fusion(f32[2,256,64,4,4]{2,4,3,1,0:T(4,128)} %fusion, f32[2,256,64,4,4]{2,4,3,1,0:T(4,128)} %fusion.2, f32[64,4,2,4,256]{0,3,1,4,2:T(4,128)S(1)} %copy-done.1, f32[64,64,2,256]{1,0,3,2:T(8,128)} %bitcast.251, f32[64,64,2,256]{1,0,3,2:T(8,128)} %bitcast.252, f32[64,64,2,256]{1,0,3,2:T(8,128)} %bitcast.253, ...), kind=kOutput, calls=%fused_computation.63 | convolution fusion | flops 417333248 | bytes 33590320 | tf_op jit(solution)/shard_map/ilarx,ijax->jlarx/dot_general | solution.py:96
  1093.1 31.8 %all_to_all.51 = f32[64,4,8,256]{3,2,1,0:T(8,128)S(1)} all-to-all(f32[64,4,8,256]{3,2,1,0:T(8,128)S(1)} %copy.244), channel_id=1, replica_groups=mesh['task'=4,'patch'=32] {'task'}, dimensions={0} | all-to-all | bytes 4194304 | tf_op jit(solution)/shard_map/all_to_all | solution.py:228
  (270 shorter events, 409.5 us)
Async XLA Ops:
  2.4 25.3 %collective-permute-start.12 = (f32[4,8192]{1,0:T(4,128)}, f32[4,8192]{1,0:T(4,128)}, u32[]{:S(2)}, u32[]{:S(2)}) collective-permute-start(f32[4,8192]{1,0:T(4,128)} %pad_maximum_fusion.18), channel_id=1, source_target_pairs={{0,2},{1,3},{2,4},{3,5},{4,6},{5,7},{6,8},{7,9},{8,10},{9,11},{10,... | collective-permute-start | bytes 393224 | tf_op jit(solution)/shard_map/ppermute | solution.py:33
  6.7 36.0 %collective-permute-start.13 = (f32[4,8192]{1,0:T(4,128)}, f32[4,8192]{1,0:T(4,128)}, u32[]{:S(2)}, u32[]{:S(2)}) collective-permute-start(f32[4,8192]{1,0:T(4,128)} %pad_maximum_fusion.18), channel_id=1, source_target_pairs={{0,1},{1,2},{2,3},{3,4},{4,5},{5,6},{6,7},{7,8},{8,9},{9,10},{10,1... | collective-permute-start | bytes 393224 | tf_op jit(solution)/shard_map/ppermute | solution.py:33
  8.8 258.8 %collective-permute-start.14 = (f32[4,8192]{1,0:T(4,128)}, f32[4,8192]{1,0:T(4,128)}, u32[]{:S(2)}, u32[]{:S(2)}) collective-permute-start(f32[4,8192]{1,0:T(4,128)} %pad_maximum_fusion.18), channel_id=1, source_target_pairs={{1,0},{2,1},{3,2},{4,3},{5,4},{6,5},{7,6},{8,7},{9,8},{10,9},{11,1... | collective-permute-start | bytes 393224 | tf_op jit(solution)/shard_map/ppermute | solution.py:33
  13.6 9.7 collective-permute-start
  14.9 9.7 collective-permute-start.1
  19.6 38.8 %copy-start.27 = (pred[4,8,1024]{2,1,0:T(8,128)(4,1)}, pred[4,8,1024]{2,1,0:T(8,128)(4,1)S(1)}, u32[]{:S(2)}) copy-start(pred[4,8,1024]{2,1,0:T(8,128)(4,1)S(1)} %get-tuple-element.45) | copy-start | bytes 98308
  19.6 38.8 %copy-start.29 = (pred[4,8,1024]{2,1,0:T(8,128)(4,1)}, pred[4,8,1024]{2,1,0:T(8,128)(4,1)S(1)}, u32[]{:S(2)}) copy-start(pred[4,8,1024]{2,1,0:T(8,128)(4,1)S(1)} %get-tuple-element.46) | copy-start | bytes 98308
  19.6 38.8 %copy-start.31 = (pred[4,8,1024]{2,1,0:T(8,128)(4,1)}, pred[4,8,1024]{2,1,0:T(8,128)(4,1)S(1)}, u32[]{:S(2)}) copy-start(pred[4,8,1024]{2,1,0:T(8,128)(4,1)S(1)} %get-tuple-element.47) | copy-start | bytes 98308
  20.6 35.4 %copy-start.26 = (f32[8,1024]{1,0:T(8,128)}, f32[8,1024]{1,0:T(8,128)S(1)}, u32[]{:S(2)}) copy-start(f32[8,1024]{1,0:T(8,128)S(1)} %convert_element_type.39) | copy-start | bytes 98308
  23.3 35.2 %copy-start.22 = (f32[4,8,1024]{2,1,0:T(8,128)}, f32[4,8,1024]{2,1,0:T(8,128)S(1)}, u32[]{:S(2)}) copy-start(f32[4,8,1024]{2,1,0:T(8,128)S(1)} %broadcast_subtract_fusion.1) | copy-start | bytes 393220
  23.3 245.2 %collective-permute-start.15 = (f32[4,8192]{1,0:T(4,128)}, f32[4,8192]{1,0:T(4,128)}, u32[]{:S(2)}, u32[]{:S(2)}) collective-permute-start(f32[4,8192]{1,0:T(4,128)} %pad_maximum_fusion.18), channel_id=1, source_target_pairs={{2,0},{3,1},{4,2},{5,3},{6,4},{7,5},{8,6},{9,7},{10,8},{11,9},{12,... | collective-permute-start | bytes 393224 | tf_op jit(solution)/shard_map/ppermute | solution.py:33
  26.4 6.5 collective-permute-start.2
  27.7 5.4 collective-permute-start.3
  34.9 8.7 collective-permute-start.4
  36.2 7.6 collective-permute-start.5
  45.6 8.9 collective-permute-start.6
  46.9 8.3 collective-permute-start.7
  262.4 28.7 %all-to-all-start = ((f32[4,1,131072]{2,1,0:T(1,128)}), f32[4,1,131072]{2,1,0:T(1,128)}, u32[]{:S(2)}, u32[]{:S(2)}) async-start(f32[4,1,131072]{2,1,0:T(1,128)} %reshape.262), calls=%async_computation | async-start | bytes 4194304 | tf_op jit(solution)/shard_map/all_to_all | solution.py:147
  360.9 119.9 %collective-permute-start.8 = (f32[64,8192]{1,0:T(8,128)}, f32[64,8192]{1,0:T(8,128)}, u32[]{:S(2)}, u32[]{:S(2)}) collective-permute-start(f32[64,8192]{1,0:T(8,128)} %bitcast.10), channel_id=1, source_target_pairs={{0,2},{1,3},{2,4},{3,5},{4,6},{5,7},{6,8},{7,9},{8,10},{9,11},{10,... | collective-permute-start | bytes 6291464 | tf_op jit(solution)/shard_map/ppermute | solution.py:33
  373.9 110.8 %collective-permute-start.9 = (f32[64,8192]{1,0:T(8,128)}, f32[64,8192]{1,0:T(8,128)}, u32[]{:S(2)}, u32[]{:S(2)}) collective-permute-start(f32[64,8192]{1,0:T(8,128)} %bitcast.10), channel_id=1, source_target_pairs={{0,1},{1,2},{2,3},{3,4},{4,5},{5,6},{6,7},{7,8},{8,9},{9,10},{10,1... | collective-permute-start | bytes 6291464 | tf_op jit(solution)/shard_map/ppermute | solution.py:33
  376.5 118.9 %collective-permute-start.10 = (f32[64,8192]{1,0:T(8,128)}, f32[64,8192]{1,0:T(8,128)}, u32[]{:S(2)}, u32[]{:S(2)}) collective-permute-start(f32[64,8192]{1,0:T(8,128)} %bitcast.10), channel_id=1, source_target_pairs={{1,0},{2,1},{3,2},{4,3},{5,4},{6,5},{7,6},{8,7},{9,8},{10,9},{11,1... | collective-permute-start | bytes 6291464 | tf_op jit(solution)/shard_map/ppermute | solution.py:33
  471.1 293.8 %all-to-all-start.1 = ((f32[4,1,131072]{2,1,0:T(1,128)}), f32[4,1,131072]{2,1,0:T(1,128)}, u32[]{:S(2)}, u32[]{:S(2)}) async-start(f32[4,1,131072]{2,1,0:T(1,128)} %reshape.264), calls=%async_computation.1 | async-start | bytes 4194304 | tf_op jit(solution)/shard_map/all_to_all | solution.py:146
  479.4 50.4 %collective-permute-start.11 = (f32[64,8192]{1,0:T(8,128)}, f32[64,8192]{1,0:T(8,128)S(1)}, u32[]{:S(2)}, u32[]{:S(2)}) collective-permute-start(f32[64,8192]{1,0:T(8,128)} %bitcast.10), channel_id=1, source_target_pairs={{2,0},{3,1},{4,2},{5,3},{6,4},{7,5},{8,6},{9,7},{10,8},{11,9},{12,... | collective-permute-start | bytes 6291464 | tf_op jit(solution)/shard_map/ppermute | solution.py:33
  730.5 11.8 %collective-permute-start.17 = (f32[64,64,2,1]{1,0,3,2:T(8,128)S(1)}, f32[64,64,2,1]{1,0,3,2:T(8,128)S(1)}, u32[]{:S(2)}, u32[]{:S(2)}) collective-permute-start(f32[64,64,2,1]{1,0,3,2:T(8,128)S(1)} %get-tuple-element.26), channel_id=1, source_target_pairs={{32,0},{64,32},{96,64},{33,1},{65,33},{97,65},{34,2},{66,34},{98,6... | collective-permute-start | bytes 98312 | tf_op jit(solution)/shard_map/ppermute | solution.py:23
  731.8 13.3 %collective-permute-start.16 = (f32[64,64,2,1]{1,0,3,2:T(8,128)S(1)}, f32[64,64,2,1]{1,0,3,2:T(8,128)S(1)}, u32[]{:S(2)}, u32[]{:S(2)}) collective-permute-start(f32[64,64,2,1]{1,0,3,2:T(8,128)S(1)} %get-tuple-element.25), channel_id=1, source_target_pairs={{0,32},{32,64},{64,96},{1,33},{33,65},{65,97},{2,34},{34,66},{66,9... | collective-permute-start | bytes 98312 | tf_op jit(solution)/shard_map/ppermute | solution.py:21
  758.3 44.9 %collective-permute-start.18 = (f32[64,64,1,66]{3,1,2,0:T(8,128)}, f32[64,64,1,66]{3,1,2,0:T(8,128)}, u32[]{:S(2)}, u32[]{:S(2)}) collective-permute-start(f32[64,64,1,66]{3,1,2,0:T(8,128)} %get-tuple-element.23), channel_id=1, source_target_pairs={{0,1},{1,2},{2,3},{3,4},{4,5},{5,6},{6,7},{7,8},{8,9},{9,10},{10,1... | collective-permute-start | bytes 3244040 | tf_op jit(solution)/shard_map/ppermute | solution.py:21
  761.2 42.0 %collective-permute-start.19 = (f32[64,64,1,66]{3,1,2,0:T(8,128)}, f32[64,64,1,66]{3,1,2,0:T(8,128)}, u32[]{:S(2)}, u32[]{:S(2)}) collective-permute-start(f32[64,64,1,66]{3,1,2,0:T(8,128)} %get-tuple-element.24), channel_id=1, source_target_pairs={{1,0},{2,1},{3,2},{4,3},{5,4},{6,5},{7,6},{8,7},{9,8},{10,9},{11,1... | collective-permute-start | bytes 3244040 | tf_op jit(solution)/shard_map/ppermute | solution.py:23
  1093.0 32.1 %copy-start.13 = (f32[16,8,1024]{2,1,0:T(8,128)S(1)}, f32[16,8,1024]{2,1,0:T(8,128)}, u32[]{:S(2)}) copy-start(f32[16,8,1024]{2,1,0:T(8,128)} %copy-done.12) | copy-start | bytes 1572868
  1093.0 32.1 %copy-start.15 = (f32[16,8,1024]{2,1,0:T(8,128)S(1)}, f32[16,8,1024]{2,1,0:T(8,128)}, u32[]{:S(2)}) copy-start(f32[16,8,1024]{2,1,0:T(8,128)} %copy-done.14) | copy-start | bytes 1572868
  1093.0 32.1 %copy-start.17 = (f32[16,8,1024]{2,1,0:T(8,128)S(1)}, f32[16,8,1024]{2,1,0:T(8,128)}, u32[]{:S(2)}) copy-start(f32[16,8,1024]{2,1,0:T(8,128)} %copy-done.16) | copy-start | bytes 1572868
  1093.0 32.1 %copy-start.19 = (f32[16,8,1024]{2,1,0:T(8,128)S(1)}, f32[16,8,1024]{2,1,0:T(8,128)}, u32[]{:S(2)}) copy-start(f32[16,8,1024]{2,1,0:T(8,128)} %copy-done.18) | copy-start | bytes 1572868
  1093.0 32.1 %copy-start.21 = (f32[4,8,1024]{2,1,0:T(8,128)S(1)}, f32[4,8,1024]{2,1,0:T(8,128)}, u32[]{:S(2)}) copy-start(f32[4,8,1024]{2,1,0:T(8,128)} %param.16) | copy-start | bytes 393220
  (38 other events, 431.4 us)
where the time goes:
time: 1150 us; the launch traced here: 1130 us
  local copies, waits for them, and re-layouts  491 us (43%)
  other arithmetic  284 us (25%)
  matrix products  198 us (17%)
  starting transfers between devices  74.1 us (6%)
  waiting for transfers between devices  46.6 us (4%)
  blocking collectives  31.8 us (3%)
    unnamed x2, other arithmetic  147 us
    unnamed x109, local copies, waits for them, and re-layouts  101 us
    mul x15, local copies, waits for them, and re-layouts, blend_weights(): row_weights[..., col_shift:col_shift + coarse_cols, None]  87.9 us
    dot_general x3, matrix products, blend_weights(): jnp.einsum('ilarx,ijax->jlarx', departure_rows, column_weights, precision...  81.1 us
    slice x8, local copies, waits for them, and re-layouts, blend_weights(): row_weights[..., col_shift:col_shift + coarse_cols, None]  43.4 us
    dot_general x6, matrix products, point_weights(): jnp.einsum('ijp,jkp->ikp', middle, inverse_root, precision=lax.Precision....  32.8 us
    dot_general x6, matrix products, point_weights(): jnp.einsum('ijp,jkp->ikp', inverse_root, root_iter, precision=lax.Precisi...  32.5 us
    all_to_all x1, blocking collectives, body(): lax.all_to_all(kalman_adjustment, 'task', split_axis=0, concat_axis=3, ti...  31.8 us
  transfers between devices with their start and end apart: 22, of which 5 were waited for; matrix products, arithmetic and copies ran while one was open for 54% of the time, Pallas kernels for 0%

commit v1 on v0

v1 whole, which is shorter than its diff:
```python
import functools

import jax
import jax.numpy as jnp
from jax import lax
from jax.experimental import pallas as pl
from jax.experimental.pallas import tpu as pltpu
from jax.sharding import PartitionSpec as P

MESH = pl.DeviceIdType.MESH
F32 = jnp.float32
BF16 = jnp.bfloat16
STEPS = 4
NS_ITERS = 6
TASKS = 4
STRIPS = 32
GROUP = 4
SPAN = 276
LIMIT = 58 * 1024 * 1024


def iota(shape, dim):
    return lax.broadcasted_iota(jnp.int32, shape, dim)


def split(x):
    hi = x.astype(BF16)
    return hi, (x - hi.astype(F32)).astype(BF16)


def greet(peers):
    barrier = pltpu.get_barrier_semaphore()
    for peer in peers:
        pl.semaphore_signal(barrier, inc=1, device_id=peer, device_id_type=MESH)
    pl.semaphore_wait(barrier, len(peers))


def forecast_kernel(
    x, wet, donor, frac, rate, attr,
    w5, f1, e5, attr5,
    hal, whal, fs0, fs1, es,
    halo_s, halo_r, wet_s, wet_r, attr_s, attr_r, own, swap_s, swap_r, win_s, win_r, edge_s, edge_r,
):
    t = lax.axis_index("task")
    s = lax.axis_index("patch")
    strip = {d: lax.rem(s + d + STRIPS, STRIPS) for d in (-2, -1, 1, 2)}
    peer = {k: lax.rem(t + k, TASKS) for k in range(TASKS)}
    greet([(t, strip[d]) for d in (-2, -1, 1, 2)] + [(peer[k], s) for k in (1, 2, 3)])

    def send(src, dst, ss, rs, to):
        copy = pltpu.make_async_remote_copy(
            src_ref=src, dst_ref=dst, send_sem=ss, recv_sem=rs, device_id=to, device_id_type=MESH
        )
        copy.start()
        return copy

    wet_copies = []
    halo_copies = []
    for i, d in enumerate((-1, 1)):
        part = pl.ds(4 * i, 4)
        wet_copies.append(
            send(wet.at[part], whal.at[part], wet_s.at[i], wet_r.at[i], (t, strip[d]))
        )
    for c in range(4):
        members = pl.ds(4 * c, 4)
        for i, d in enumerate((-1, 1)):
            part = pl.ds(4 * i, 4)
            halo_copies.append(
                send(
                    x.at[members, :, part],
                    hal.at[members, :, part],
                    halo_s.at[2 * c + i],
                    halo_r.at[2 * c + i],
                    (t, strip[d]),
                )
            )
    attr_copies = [
        send(attr, attr5.at[2 - d], attr_s.at[i], attr_r.at[i], (t, strip[d]))
        for i, d in enumerate((-2, -1, 1, 2))
    ]
    own_attr = pltpu.make_async_copy(attr, attr5.at[2], own.at[0])
    own_attr.start()

    sub = iota((8, 1024), 0)
    col = iota((8, 1024), 1)
    lane = iota((8, 128), 1)
    below = jnp.where(s < STRIPS - 1, 1.0, 0.0)
    above = jnp.where(s > 0, 1.0, 0.0)
    inside = jnp.where(sub < 4, below, above)
    for copy in wet_copies:
        copy.wait()
    ocean = wet[...].astype(F32)
    ocean_halo = whal[...].astype(F32) * inside
    es[...] = jnp.zeros_like(es)

    def member(m, carry):
        levels = []
        for lev in range(4):
            here = x[m, lev]
            out = hal[m, lev] * inside
            k = rate[lev]
            for step in range(STEPS):
                east_h = jnp.where(col == 1023, 0.0, pltpu.roll(here, 1023, 1))
                west_h = jnp.where(col == 0, 0.0, pltpu.roll(here, 1, 1))
                down_h, down_o = pltpu.roll(here, 1, 0), pltpu.roll(out, 1, 0)
                up_h, up_o = pltpu.roll(here, 7, 0), pltpu.roll(out, 7, 0)
                beside = (
                    jnp.where(sub == 7, up_o, up_h)
                    + jnp.where(sub == 0, down_o, down_h)
                    + east_h
                    + west_h
                )
                new = ocean * (here + k * (beside - 4.0 * here))
                if step < STEPS - 1:
                    east_o = jnp.where(col == 1023, 0.0, pltpu.roll(out, 1023, 1))
                    west_o = jnp.where(col == 0, 0.0, pltpu.roll(out, 1, 1))
                    beside = (
                        jnp.where(sub == 7, up_h, up_o)
                        + jnp.where(sub == 0, down_h, down_o)
                        + east_o
                        + west_o
                    )
                    out = ocean_halo * (out + k * (beside - 4.0 * out))
                here = new
            levels.append(here)
        for lev in range(4):
            tier = donor[lev]
            low = jnp.where(tier == 0, levels[0], jnp.where(tier == 1, levels[1], levels[2]))
            high = jnp.where(tier == 0, levels[1], jnp.where(tier == 1, levels[2], levels[3]))
            share = frac[lev]
            result = (1.0 - share) * low + share * high
            if lev:
                fs1[m, lev - 1] = result
            else:
                fs0[m] = result
                for k in range(TASKS):
                    right = result[:, 256 * (k + 1) % 1024 : 256 * (k + 1) % 1024 + 128]
                    left = result[:, (256 * k - 128) % 1024 : (256 * k - 128) % 1024 + 128]
                    rim = pltpu.roll(jnp.where(lane >= 124, left, right), m * 8 + 4, 1)
                    es[k] = jnp.where(lane // 8 == m, rim, es[k])
        return carry

    for c in range(4):
        halo_copies[2 * c].wait_recv()
        halo_copies[2 * c + 1].wait_recv()
        lax.fori_loop(4 * c, 4 * c + 4, member, 0)

    mine = pl.ds(pl.multiple_of(16 * t, 16), 16)
    local = []
    swaps = {}
    here_cols = pl.ds(pl.multiple_of(256 * t, 256), 256)
    for n, (src, dst) in enumerate(
        [
            (fs0.at[:, :, here_cols], w5.at[2, mine]),
            (es.at[t], e5.at[2, t]),
            (fs1.at[:, :, :, here_cols], f1.at[mine]),
        ]
    ):
        copy = pltpu.make_async_copy(src, dst, own.at[1 + n])
        copy.start()
        local.append(copy)
    for n in range(3):
        for k in (1, 2, 3):
            to = peer[k]
            cols = pl.ds(pl.multiple_of(256 * to, 256), 256)
            src, dst = (
                (fs0.at[:, :, cols], w5.at[2, mine]),
                (es.at[to], e5.at[2, t]),
                (fs1.at[:, :, :, cols], f1.at[mine]),
            )[n]
            i = 3 * n + k - 1
            swaps[n, k] = send(src, dst, swap_s.at[i], swap_r.at[i], (to, s))

    windows = []
    for k in range(TASKS):
        if k:
            swaps[0, k].wait_recv()
        else:
            local[0].wait()
        src = lax.rem(t - k + TASKS, TASKS)
        part = pl.ds(pl.multiple_of(16 * src, 16), 16)
        for i, d in enumerate((-2, 2, -1, 1)):
            n = 4 * k + i
            windows.append(
                send(w5.at[2, part], w5.at[2 - d, part], win_s.at[n], win_r.at[n], (t, strip[d]))
            )
    local[1].wait()
    for k in (1, 2, 3):
        swaps[1, k].wait_recv()
    for i, d in enumerate((-2, 2, -1, 1)):
        windows.append(
            send(e5.at[2], e5.at[2 - d], edge_s.at[i], edge_r.at[i], (t, strip[d]))
        )
    for copy in windows + attr_copies:
        copy.wait()
    own_attr.wait()
    local[2].wait()
    for (n, k), copy in swaps.items():
        copy.wait_send()
        if n == 2:
            copy.wait_recv()
    for copy in halo_copies:
        copy.wait_send()


def forecast(x, wet, donor, frac, rate, attr):
    dma = pltpu.SemaphoreType.DMA
    vmem = pl.BlockSpec(memory_space=pltpu.VMEM)
    anywhere = pl.BlockSpec(memory_space=pl.ANY)
    return pl.pallas_call(
        forecast_kernel,
        out_shape=[
            jax.ShapeDtypeStruct((5, 64, 8, 256), F32),
            jax.ShapeDtypeStruct((64, 3, 8, 256), F32),
            jax.ShapeDtypeStruct((5, 4, 8, 128), F32),
            jax.ShapeDtypeStruct((5, 3, 32, 128), F32),
        ],
        in_specs=[vmem, vmem, vmem, vmem, pl.BlockSpec(memory_space=pltpu.SMEM), vmem],
        out_specs=[anywhere] * 4,
        scratch_shapes=[
            pltpu.VMEM((16, 4, 8, 1024), F32),
            pltpu.VMEM((8, 1024), jnp.int32),
            pltpu.VMEM((16, 8, 1024), F32),
            pltpu.VMEM((16, 3, 8, 1024), F32),
            pltpu.VMEM((4, 8, 128), F32),
            dma((8,)), dma((8,)), dma((2,)), dma((2,)), dma((4,)), dma((4,)),
            dma((4,)), dma((9,)), dma((9,)), dma((16,)), dma((16,)), dma((4,)), dma((4,)),
        ],
        compiler_params=pltpu.CompilerParams(
            collective_id=0, has_side_effects=True, vmem_limit_bytes=LIMIT
        ),
    )(x, wet, donor, frac, rate, attr)


def spread(x, shift):
    lane = iota(x.shape, 1)
    return jnp.where(
        lane < 64, pltpu.roll(x, (127 - shift) % 128, 1), pltpu.roll(x, 63 - shift, 1)
    )


def doubled(x):
    hi, lo = split(x)
    left = iota(x.shape, 1) < 64
    zero = jnp.zeros((64, 128), BF16)

    def diagonal(y):
        y = y.astype(F32)
        return jnp.concatenate(
            [jnp.where(left, y, 0.0), jnp.where(left, 0.0, y)], axis=0
        ).astype(BF16)

    hi, lo = diagonal(hi), diagonal(lo)
    zero = jnp.zeros((128, 128), BF16)
    return jnp.concatenate(
        [jnp.concatenate([hi, lo], axis=1), jnp.concatenate([hi, zero], axis=1)], axis=0
    )


def times(x, weights):
    hi, lo = split(x)
    product = jnp.dot(
        jnp.concatenate([hi, lo], axis=1), weights, preferred_element_type=F32
    )
    return product[:, :128] + product[:, 128:]


def weights_kernel(w5, e5, attr, code, out, cols, rim, mean, picked, base, taper, force, system, drive):
    lane = iota((8, 128), 1)
    sub = iota((8, 128), 0)

    def place(st, carry):
        for src in range(TASKS):
            tile = e5[st, src]
            for m in range(16):
                rim[16 * src + m] = pltpu.roll(tile, (128 - 8 * m) % 128, 1) if m else tile
        rows = pl.ds(pl.multiple_of(8 * st, 8), 8)
        means, rim_means = [], []
        for r in range(8):
            whole = w5[st, :, r, :]
            mu = jnp.sum(whole, axis=0, keepdims=True) * (1.0 / 64)
            dev = whole - mu
            cols[4:260, st, r, :] = jnp.concatenate([dev, dev], axis=0).T
            means.append(mu)
            whole = rim[:, r, :]
            mu = jnp.sum(whole, axis=0, keepdims=True) * (1.0 / 64)
            dev = whole - mu
            turned = jnp.concatenate([dev, dev], axis=0).T
            cols[0:4, st, r, :] = turned[0:4]
            cols[260:264, st, r, :] = turned[4:8]
            rim_means.append(mu)
        mean[rows, 0:256] = jnp.concatenate(means, axis=0)
        mean[rows, 256:384] = jnp.concatenate(rim_means, axis=0)
        return carry

    lax.fori_loop(0, 5, place, 0)

    spot = iota((384, 128), 0)
    coarse = iota((384, 128), 1)
    lane_of = iota((40, 384), 1)
    known = jnp.where(lane_of < 264, mean[...], 0.0)
    for q in range(4):
        want = jnp.where(
            coarse == 0, 256 + q, jnp.where(coarse == 65, 260 + q, 4 * coarse - 4 + q)
        )
        picked[q] = jnp.dot(
            known,
            jnp.where((spot == want) & (coarse < 66), 1.0, 0.0),
            precision=lax.Precision.HIGHEST,
            preferred_element_type=F32,
        )
    for slot in range(32):
        base[slot] = jnp.broadcast_to(code[slot : slot + 1, :], (8, 128)) - sub

    point_row = jnp.where(lane < 64, 1.5, 5.5)
    height = sub.astype(F32)
    taper[45] = jnp.zeros((8, 128), F32)

    def weigh(st, carry):
        for cr in range(9):
            q, shift = (cr - 4) % 4, (cr - 4) // 4
            row = spread(attr[st, 0, 8 * q : 8 * q + 8, :], shift)
            value = spread(attr[st, 1, 8 * q : 8 * q + 8, :], shift)
            var = spread(attr[st, 2, 8 * q : 8 * q + 8, :], shift)
            tile = (st * 9 + cr) * 8
            count = jnp.zeros((8, 128), F32)
            for slot in range(32):
                count = count + jnp.where(base[slot] == tile, 1.0, 0.0)
            apart = row + (8.0 * (st - 2).astype(F32)) - point_row
            dist = apart * apart + (cr - 5.5) ** 2
            weight = count * jnp.exp(dist * (-1.0 / 1152.0)) / var
            pull = weight * value
            total = jnp.zeros((8, 128), F32)
            pulled = jnp.zeros((8, 128), F32)
            for k in range(8):
                hit = row[k : k + 1] == height
                total = total + jnp.where(hit, weight[k : k + 1], 0.0)
                pulled = pulled + jnp.where(hit, pull[k : k + 1], 0.0)
            centre = spread(picked[q, pl.ds(pl.multiple_of(8 * st, 8), 8), :], shift)
            taper[cr * 5 + st] = total
            force[cr * 5 + st] = pulled - total * centre
        return carry

    lax.fori_loop(0, 5, weigh, 0)

    tall_lane = iota((368, 128), 1)
    eye = jnp.where(iota((64, 128), 0) == iota((64, 128), 1) % 64, 1.0, 0.0)

    def gram(b, carry):
        index = jnp.where(lane < 64, b, 64 + b)
        near = cols[pl.ds(4 * b, 10)].reshape(400, 128)[:368]
        spread_taper = jnp.concatenate(
            [jnp.take_along_axis(taper[k], index, axis=1) for k in range(46)], axis=0
        )
        spread_force = jnp.concatenate(
            [jnp.take_along_axis(force[k], index, axis=1) for k in range(45)], axis=0
        )
        s_hi, s_lo = split(near * spread_taper)
        n_hi = near.astype(BF16).astype(F32)
        both = jnp.where(tall_lane < 64, n_hi, near - n_hi).astype(BF16)
        product = lax.dot_general(
            both,
            jnp.concatenate([s_hi, s_lo], axis=1),
            (((0,), (0,)), ((), ())),
            preferred_element_type=F32,
        )
        product = product[:64] + product[64:]
        system[b] = product[:, :128] + product[:, 128:] + 63.0 * eye
        drive[b] = jnp.broadcast_to(
            jnp.sum(near[:360] * spread_force, axis=0, keepdims=True), (8, 128)
        )
        return carry

    lax.fori_loop(0, 64, gram, 0)

    half = iota((64, 128), 1) < 64

    def solve(n, carry):
        pairs = [n * GROUP + k for k in range(GROUP)]
        roots, inverses, norms = [], [], []
        for b in pairs:
            x = system[b]
            squares = jnp.sum(x * x, axis=0, keepdims=True)
            left = iota((1, 128), 1) < 64
            one = jnp.sum(jnp.where(left, squares, 0.0), axis=1, keepdims=True)
            two = jnp.sum(jnp.where(left, 0.0, squares), axis=1, keepdims=True)
            norm = jnp.sqrt(jnp.where(left, one, two))
            norms.append(norm)
            roots.append(x / norm)
            inverses.append(None)
        for turn in range(NS_ITERS):
            middles = []
            for k in range(GROUP):
                if turn == 0:
                    middles.append(1.5 * eye - 0.5 * roots[k])
                else:
                    middles.append(1.5 * eye - 0.5 * times(inverses[k], doubled(roots[k])))
            for k in range(GROUP):
                weights = doubled(middles[k])
                if turn == 0:
                    inverses[k] = middles[k]
                    roots[k] = times(roots[k], weights)
                elif turn < NS_ITERS - 1:
                    both = times(jnp.concatenate([roots[k], inverses[k]], axis=0), weights)
                    roots[k], inverses[k] = both[:64], both[64:]
                else:
                    inverses[k] = times(inverses[k], weights)
        finals = []
        for k, b in enumerate(pairs):
            weights = doubled(inverses[k])
            drift = times(times(drive[b], weights), weights)[:1] / norms[k]
            on_diagonal = eye * drift
            one = jnp.sum(jnp.where(half, on_diagonal, 0.0), axis=1, keepdims=True)
            two = jnp.sum(jnp.where(half, 0.0, on_diagonal), axis=1, keepdims=True)
            finals.append(
                jnp.sqrt(63.0 / norms[k]) * inverses[k] + jnp.where(half, one, two)
            )
        for k in range(0, GROUP, 2):
            g = n * (GROUP // 2) + k // 2
            out[0, g] = jnp.where(half, finals[k], pltpu.roll(finals[k + 1], 64, 1))
            out[1, g] = jnp.where(half, pltpu.roll(finals[k], 64, 1), finals[k + 1])
        return carry

    lax.fori_loop(0, 64 // GROUP, solve, 0)


def point_weights(w5, e5, attr5, code):
    vmem = pl.BlockSpec(memory_space=pltpu.VMEM)
    return pl.pallas_call(
        weights_kernel,
        out_shape=jax.ShapeDtypeStruct((2, 32, 64, 128), F32),
        in_specs=[vmem] * 4,
        out_specs=vmem,
        scratch_shapes=[
            pltpu.VMEM((264, 5, 8, 128), F32),
            pltpu.VMEM((64, 8, 128), F32),
            pltpu.VMEM((40, 384), F32),
            pltpu.VMEM((4, 40, 128), F32),
            pltpu.VMEM((32, 8, 128), jnp.int32),
            pltpu.VMEM((46, 8, 128), F32),
            pltpu.VMEM((45, 8, 128), F32),
            pltpu.VMEM((64, 64, 128), F32),
            pltpu.VMEM((64, 8, 128), F32),
        ],
        compiler_params=pltpu.CompilerParams(vmem_limit_bytes=LIMIT),
    )(w5, e5, attr5, code)


def hat(x):
    return jnp.maximum(1.0 - jnp.abs(x - 1.5) * 0.25, 0.0)


def analysis_kernel(
    weights, w5, f1, wet,
    out,
    every, f0, turned, total, result,
    own, side_s, side_r, row_s, row_r, corner_s, corner_r, back_s, back_r,
):
    t = lax.axis_index("task")
    s = lax.axis_index("patch")
    up, down = lax.rem(s + STRIPS - 1, STRIPS), lax.rem(s + 1, STRIPS)
    peer = {k: lax.rem(t + k, TASKS) for k in range(TASKS)}
    right, left = peer[1], peer[3]
    load = pltpu.make_async_copy(w5.at[2], f0, own.at[0])
    load.start()
    greet(
        [(peer[k], s) for k in (1, 2, 3)]
        + [(t, up), (t, down)]
        + [(x, y) for x in (right, left) for y in (up, down)]
    )

    def send(src, dst, ss, rs, to):
        copy = pltpu.make_async_remote_copy(
            src_ref=src, dst_ref=dst, send_sem=ss, recv_sem=rs, device_id=to, device_id_type=MESH
        )
        copy.start()
        return copy

    copies = []
    for i, (to, mine, there) in enumerate([(right, 31, 0), (left, 0, 33)]):
        for a in range(2):
            copies.append(
                send(
                    weights.at[a, mine], every.at[1 + a, there],
                    side_s.at[2 * i + a], side_r.at[2 * i + a], (to, s),
                )
            )
            copies.append(
                send(
                    weights.at[a, mine], every.at[3 - 3 * a, there],
                    corner_s.at[2 * i + a], corner_r.at[2 * i + a], (to, (up, down)[a]),
                )
            )
    for a in range(2):
        copies.append(
            send(
                weights.at[a], every.at[3 - 3 * a, pl.ds(1, 32)],
                row_s.at[a], row_r.at[a], (t, (up, down)[a]),
            )
        )

    total[...] = jnp.zeros_like(total)
    load.wait()
    lane_wide = iota((256, 128), 1) < 64
    cols = pl.ds(pl.multiple_of(256 * t, 256), 256)

    def field(lev, r):
        return f0[:, r, :] if lev == 0 else f1[:, lev - 1, r, :]

    def deviation(lev, r):
        whole = field(lev, r)
        return whole - jnp.sum(whole, axis=0, keepdims=True) * (1.0 / 64)

    for lev in range(4):
        for r in range(8):
            dev = deviation(lev, r)
            both = jnp.concatenate([dev, dev], axis=0).T
            high = both.astype(BF16).astype(F32)
            turned[10:266, r // 2, 4 * (r % 2) + lev, :] = jnp.where(
                lane_wide, high, both - high
            )

    lane = iota((8, 128), 1)
    sub = iota((8, 128), 0)
    second = jnp.where(lane < 64, 0.0, 4.0)
    top = jnp.where(s == 0, 1.0, 0.0)
    bottom = jnp.where(s == STRIPS - 1, 1.0, 0.0)

    def row_share(a, k):
        r = (2 * k + sub // 4).astype(F32)
        if a == -1:
            return hat(r + 4.0) * (1.0 - top)
        if a == 0:
            return hat(r) + hat(r + 4.0) * top
        if a == 1:
            return hat(r - 4.0) + hat(r - 8.0) * bottom
        return hat(r - 8.0) * (1.0 - bottom)

    def col_share(g):
        first = jnp.where((g == 0) & (t == 0), 1.0, 0.0)
        last = jnp.where((g == 31) & (t == TASKS - 1), 1.0, 0.0)
        alive = jnp.where(
            ((g == -1) & (t == 0)) | ((g == 32) & (t == TASKS - 1)), 0.0, 1.0
        )
        shares = []
        for c in range(12):
            x = (c - 2.0) - second
            share = hat(x)
            if c in (2, 3):
                share = share + jnp.where(lane < 64, hat(x + 4.0), 0.0) * first
            if c in (8, 9):
                share = share + jnp.where(lane < 64, 0.0, hat(x - 4.0)) * last
            shares.append(share * alive)
        return shares

    def paired(x):
        hi, lo = split(x)
        zero = jnp.zeros((64, 128), BF16)
        return jnp.concatenate(
            [jnp.concatenate([hi, lo], axis=1), jnp.concatenate([hi, zero], axis=1)], axis=0
        )

    def add(g, a, operand, first, count, shares):
        rows = turned[pl.ds(8 * g + 8, 12), first : first + count]
        rows = rows.reshape(12 * count * 8, 128).astype(BF16)
        product = jnp.dot(rows, paired(operand), preferred_element_type=F32)
        product = (product[:, :128] + product[:, 128:]).reshape(12, count, 8, 128)
        parts = []
        for c in range(12):
            parts.append(
                jnp.stack(
                    [product[c, k] * row_share(a, first + k) * shares[c] for k in range(count)]
                )
            )
        total[pl.ds(8 * g + 8, 12), first : first + count] += jnp.stack(parts)

    def inner(g, carry):
        shares = col_share(g)
        add(g, 0, weights[0, g], 0, 3, shares)
        add(g, 1, weights[1, g], 1, 3, shares)
        return carry

    lax.fori_loop(0, 32, inner, 0)

    for copy in copies:
        copy.wait()

    for g in (-1, 32):
        shares = col_share(g)
        add(g, 0, every[1, g + 1], 0, 3, shares)
        add(g, 1, every[2, g + 1], 1, 3, shares)

    def outer(n, carry):
        g = n - 1
        shares = col_share(g)
        add(g, -1, every[0, n], 0, 1, shares)
        add(g, 2, every[3, n], 3, 1, shares)
        return carry

    lax.fori_loop(0, 34, outer, 0)

    for r in range(8):
        ocean = wet[r : r + 1, cols].astype(F32)
        for lev in range(4):
            back = total[10:266, r // 2, 4 * (r % 2) + lev, :].T
            blended = back[:64] + back[64:]
            result[:, lev, r, :] = field(lev, r) + ocean * (blended - deviation(lev, r))

    mine = pl.ds(pl.multiple_of(16 * t, 16), 16)
    keep = pltpu.make_async_copy(result.at[mine], out.at[:, :, :, cols], own.at[1])
    keep.start()
    copies = []
    for k in (1, 2, 3):
        theirs = pl.ds(pl.multiple_of(16 * peer[k], 16), 16)
        copies.append(
            send(
                result.at[theirs], out.at[:, :, :, cols],
                back_s.at[k - 1], back_r.at[k - 1], (peer[k], s),
            )
        )
    for copy in copies:
        copy.wait()
    keep.wait()


def analysed(weights, w5, f1, wet):
    dma = pltpu.SemaphoreType.DMA
    vmem = pl.BlockSpec(memory_space=pltpu.VMEM)
    anywhere = pl.BlockSpec(memory_space=pl.ANY)
    return pl.pallas_call(
        analysis_kernel,
        out_shape=jax.ShapeDtypeStruct((16, 4, 8, 1024), F32),
        in_specs=[vmem, anywhere, vmem, vmem],
        out_specs=anywhere,
        scratch_shapes=[
            pltpu.VMEM((4, 34, 64, 128), F32),
            pltpu.VMEM((64, 8, 256), F32),
            pltpu.VMEM((SPAN, 4, 8, 128), F32),
            pltpu.VMEM((SPAN, 4, 8, 128), F32),
            pltpu.VMEM((64, 4, 8, 256), F32),
            dma((2,)), dma((4,)), dma((4,)), dma((2,)), dma((2,)), dma((4,)), dma((4,)),
            dma((3,)), dma((3,)),
        ],
        compiler_params=pltpu.CompilerParams(
            collective_id=1, has_side_effects=True, vmem_limit_bytes=LIMIT
        ),
    )(weights, w5, f1, wet)


def body(
    trials_initial_dye,
    diffusivity,
    wet_mask,
    deeper_donor_tier,
    shallower_tier_fraction,
    obs_pos,
    obs_value,
    obs_var,
    observation_list,
    obs_count,
):
    t = lax.axis_index("task")
    s = lax.axis_index("patch")
    facts = jnp.stack([(obs_pos // 1024).astype(F32), obs_value, obs_var])
    facts = facts.reshape(3, 256, 32).transpose(0, 2, 1)
    facts = jnp.pad(facts, ((0, 0), (0, 0), (1, 127)), constant_values=1.0)
    attr = lax.dynamic_slice_in_dim(facts, 64 * t, 128, 2)
    w5, f1, e5, attr5 = forecast(
        trials_initial_dye,
        wet_mask,
        deeper_donor_tier,
        shallower_tier_fraction,
        diffusivity,
        attr,
    )
    rel_strip = observation_list // 8192 - (s - 2)
    rel_col = observation_list % 8192 // 8 - (
        256 * t + 4 * jnp.arange(64, dtype=jnp.int32)[None, :, None] - 4
    )
    code = (rel_strip * 9 + rel_col) * 8 + observation_list % 8
    live = jnp.arange(32, dtype=jnp.int32)[None, None, :] < obs_count[:, :, None]
    code = jnp.where(live, code, -100000).reshape(128, 32).T
    weights = point_weights(w5, e5, attr5, code)
    return analysed(weights, w5, f1, wet_mask)


def solution(mesh):
    return jax.shard_map(
        body,
        mesh=mesh,
        in_specs=(
            P("task", None, "patch", None),
            P(),
            P("patch", None),
            P(None, "patch", None),
            P(None, "patch", None),
            P("patch"),
            P("patch"),
            P("patch"),
            P("patch", "task", None),
            P("patch", "task"),
        ),
        out_specs=P("task", None, "patch", None),
        check_vma=False,
    )
```

time: 1150 us -> 188 us (0.16); the launches traced: 1130 us -> 188 us
  local copies, waits for them, and re-layouts: 491 us -> 6.58 us
  other arithmetic: 284 us -> 1.63 us
  matrix products: 198 us -> 0 us
  Pallas kernels: 0 us -> 179 us
  starting transfers between devices: 74.1 us -> 0 us
  waiting for transfers between devices: 46.6 us -> 0 us
  blocking collectives: 31.8 us -> 0 us
    dot_general x24 -> x0, matrix products: 198 us -> none  [the longest x3 81.1 us: blend_weights(): jnp.einsum('ilarx,ijax->jlarx', departure_rows, column_weights, precision...]
    pallas_call x0 -> x3, Pallas kernels: none -> 179 us  [the longest x1 71 us: point_weights(): pl.pallas_call(weights_kernel, out_shape=jax.ShapeDtypeStruct((2, 32, 64,...]
    unnamed x2 -> x0, other arithmetic: 147 us -> none
    gather x6 -> x0, local copies, waits for them, and re-layouts: 140 us -> none  [the longest x1 30.1 us: body(): own_obs = jnp.take(seaface_map, obs_pos, axis=1)]
    unnamed x109 -> x1, local copies, waits for them, and re-layouts: 101 us -> 3.16 us
    mul x16 -> x0, local copies, waits for them, and re-layouts: 89.1 us -> none  [the longest x15 87.9 us: blend_weights(): row_weights[..., col_shift:col_shift + coarse_cols, None]]
    ppermute x20 -> x0, starting transfers between devices: 64.6 us -> none  [the longest x6 29.6 us: padded_2(): lax.ppermute(tail, axis, [(i, (i + 1) % count) for i in range(ends)])]
    slice x18 -> x0, local copies, waits for them, and re-layouts: 56.3 us -> none  [the longest x8 43.4 us: blend_weights(): row_weights[..., col_shift:col_shift + coarse_cols, None]]
  transfers between devices with their start and end apart: 22 -> 0, of which waited for: 5 -> 0; matrix products, arithmetic and copies ran while one was open for 54% -> 0% of each run, Pallas kernels for 0% -> 0%
where the time goes in v1:
time: 188 us
  Pallas kernels  179 us (95%)
  local copies, waits for them, and re-layouts  6.58 us (4%)
    pallas_call x1, Pallas kernels, point_weights(): pl.pallas_call(weights_kernel, out_shape=jax.ShapeDtypeStruct((2, 32, 64,...  71 us
    pallas_call x1, Pallas kernels, analysed(): pl.pallas_call(analysis_kernel, out_shape=jax.ShapeDtypeStruct((16, 4, 8,...  55.2 us
    pallas_call x1, Pallas kernels, forecast(): pl.pallas_call(forecast_kernel, out_shape=[jax.ShapeDtypeStruct((5, 64, 8...  53.1 us

profile of v1, /device:TPU:0, one launch (start us, length us, event | category | flops | bytes accessed | tf_op | source)
XLA Modules:
  0.0 187.6 jit_solution(6972466565432333504)
XLA Ops:
  0.0 0.8 fusion.7
  0.9 0.7 reshape.20
  1.6 0.8 fusion.1
  2.3 0.1 stack.12
  2.4 0.1 copy.12
  2.5 0.9 stack.13
  3.4 0.1 copy.13
  3.4 0.9 stack.14
  4.3 0.1 copy.14
  4.4 0.7 pad_dynamic-slice_fusion.attr
  5.1 53.1 %shard_map.100 = (f32[5,64,8,256]{3,2,1,0:T(8,128)}, f32[64,3,8,256]{3,2,1,0:T(8,128)}, f32[5,4,8,128]{3,2,1,0:T(8,128)}, f32[5,3,32,128]{3,2,1,0:T(8,128)}) custom-call(f32[16,4,8,1024]{3,2,1,0:T(8,128)} %x.3, s32[8,1024]{1,0:T(8,128)} %wet.3, s32[4,8,1024]{2,1,0:T(8,128)} %donor.1, f32[4,8,1024]{2,1,0:T(8,128)} %frac.1, f32[4]{0:T(128)} %rate.1, ...), custom_call_target="tpu_custom_call" | custom-call | tf_op jit(solution)/shard_map/pallas_call | solution.py:210
  58.3 71.0 %shard_map.101.weights = f32[2,32,64,128]{3,2,1,0:T(8,128)} custom-call(f32[5,64,8,256]{3,2,1,0:T(8,128)} %get-tuple-element.9.w5, f32[5,4,8,128]{3,2,1,0:T(8,128)} %get-tuple-element.10.e5, f32[5,3,32,128]{3,2,1,0:T(8,128)} %get-tuple-element.11.attr, s32[32,128]{1,0:T(8,128)} %bitcast.5), custom_call_target="tpu_custom_call" | custom-call | tf_op jit(solution)/shard_map/pallas_call | solution.py:429
  129.3 55.2 %shard_map.102 = f32[16,4,8,1024]{3,2,1,0:T(8,128)} custom-call(f32[2,32,64,128]{3,2,1,0:T(8,128)} %shard_map.101.weights, f32[5,64,8,256]{3,2,1,0:T(8,128)} %get-tuple-element.9.w5, f32[64,3,8,256]{3,2,1,0:T(8,128)} %get-tuple-element.12.f1, s32[8,1024]{1,0:T(8,128)} %wet.3), custom_call_target="tpu_custom_call" | custom-call | tf_op jit(solution)/shard_map/pallas_call | solution.py:630
  184.5 3.2 %copy.17 = f32[16,4,8,1024]{3,2,1,0:T(8,128)} copy(f32[16,4,8,1024]{3,2,1,0:T(8,128)} %shard_map.102) | data formatting | bytes 4194304
  (3 shorter events, 0.0 us)

commit v2 on v1

v2 whole, which is shorter than its diff:
```python
import functools

import jax
import jax.numpy as jnp
from jax import lax
from jax.experimental import pallas as pl
from jax.experimental.pallas import tpu as pltpu
from jax.sharding import PartitionSpec as P

MESH = pl.DeviceIdType.MESH
F32 = jnp.float32
BF16 = jnp.bfloat16
STEPS = 4
NS_ITERS = 6
TASKS = 4
STRIPS = 32
GROUP = 8
SPAN = 276
LIMIT = 58 * 1024 * 1024


def iota(shape, dim):
    return lax.broadcasted_iota(jnp.int32, shape, dim)


def split(x):
    hi = x.astype(BF16)
    return hi, (x - hi.astype(F32)).astype(BF16)


def greet(peers):
    barrier = pltpu.get_barrier_semaphore()
    for peer in peers:
        pl.semaphore_signal(barrier, inc=1, device_id=peer, device_id_type=MESH)
    pl.semaphore_wait(barrier, len(peers))


def sender(src, dst, ss, rs, to):
    return pltpu.make_async_remote_copy(
        src_ref=src, dst_ref=dst, send_sem=ss, recv_sem=rs, device_id=to, device_id_type=MESH
    )


def forecast_kernel(
    x, wet, donor, frac, rate, pos, value, var,
    w5, fs1, e5, attr5,
    hal, whal, fs0, es, attr,
    halo_s, halo_r, wet_s, wet_r, attr_s, attr_r, own, swap_s, swap_r, rim_s, rim_r,
    win_s, win_r, edge_s, edge_r,
):
    t = lax.axis_index("task")
    s = lax.axis_index("patch")
    strip = {d: lax.rem(s + d + STRIPS, STRIPS) for d in (-2, -1, 1, 2)}
    peer = {k: lax.rem(t + k, TASKS) for k in range(TASKS)}
    way = 1 - 2 * lax.rem(s, 2)
    mate = s + way
    second = lax.rem(s + 2 * way + STRIPS, STRIPS)
    other = lax.rem(s - way + STRIPS, STRIPS)
    greet([(t, strip[d]) for d in (-2, -1, 1, 2)] + [(peer[k], s) for k in (1, 2, 3)])

    def send(src, dst, ss, rs, to):
        copy = sender(src, dst, ss, rs, to)
        copy.start()
        return copy

    wet_copies = []
    halo_copies = []
    for i, d in enumerate((-1, 1)):
        part = pl.ds(4 * i, 4)
        wet_copies.append(
            send(wet.at[part], whal.at[part], wet_s.at[i], wet_r.at[i], (t, strip[d]))
        )
    for c in range(4):
        members = pl.ds(4 * c, 4)
        for i, d in enumerate((-1, 1)):
            part = pl.ds(4 * i, 4)
            halo_copies.append(
                send(
                    x.at[members, :, part],
                    hal.at[members, :, part],
                    halo_s.at[2 * c + i],
                    halo_r.at[2 * c + i],
                    (t, strip[d]),
                )
            )

    facts = jnp.concatenate(
        [(pos[...] // 1024).astype(F32).T, value[...].T, var[...].T], axis=0
    )
    spot = iota((64, 128), 0)
    coarse = iota((64, 128), 1) - 1
    gathered = jnp.zeros((96, 128), F32)
    for m in range(4):
        taken = (spot == (coarse + 4) // 4 - 1 + 16 * t) & ((coarse + 4) % 4 == m)
        rows = jnp.concatenate([facts[128 * i + 32 * m : 128 * i + 32 * m + 32] for i in range(3)])
        gathered = gathered + jnp.dot(
            rows,
            jnp.where(taken, 1.0, 0.0),
            precision=lax.Precision.HIGHEST,
            preferred_element_type=F32,
        )
    lane96 = iota((32, 128), 1)
    known = (lane96 - 1 + 64 * t >= 0) & (lane96 - 1 + 64 * t < 256)
    attr[0] = gathered[0:32]
    attr[1] = gathered[32:64]
    attr[2] = jnp.where(known, gathered[64:96], 1.0)
    own_attr = pltpu.make_async_copy(attr, attr5.at[2], own.at[0])
    own_attr.start()

    sub = iota((8, 1024), 0)
    col = iota((8, 1024), 1)
    lane = iota((8, 128), 1)
    below = jnp.where(s < STRIPS - 1, 1.0, 0.0)
    above = jnp.where(s > 0, 1.0, 0.0)
    inside = jnp.where(sub < 4, below, above)
    for copy in wet_copies:
        copy.wait()
    ocean = wet[...].astype(F32)
    ocean_halo = whal[...].astype(F32) * inside
    es[...] = jnp.zeros_like(es)

    def member(m, carry):
        levels = []
        for lev in range(4):
            here = x[m, lev]
            out = hal[m, lev] * inside
            k = rate[lev]
            for step in range(STEPS):
                east_h = jnp.where(col == 1023, 0.0, pltpu.roll(here, 1023, 1))
                west_h = jnp.where(col == 0, 0.0, pltpu.roll(here, 1, 1))
                down_h, down_o = pltpu.roll(here, 1, 0), pltpu.roll(out, 1, 0)
                up_h, up_o = pltpu.roll(here, 7, 0), pltpu.roll(out, 7, 0)
                beside = (
                    jnp.where(sub == 7, up_o, up_h)
                    + jnp.where(sub == 0, down_o, down_h)
                    + east_h
                    + west_h
                )
                new = ocean * (here + k * (beside - 4.0 * here))
                if step < STEPS - 1:
                    east_o = jnp.where(col == 1023, 0.0, pltpu.roll(out, 1023, 1))
                    west_o = jnp.where(col == 0, 0.0, pltpu.roll(out, 1, 1))
                    beside = (
                        jnp.where(sub == 7, up_h, up_o)
                        + jnp.where(sub == 0, down_h, down_o)
                        + east_o
                        + west_o
                    )
                    out = ocean_halo * (out + k * (beside - 4.0 * out))
                here = new
            levels.append(here)
        for lev in range(4):
            tier = donor[lev]
            low = jnp.where(tier == 0, levels[0], jnp.where(tier == 1, levels[1], levels[2]))
            high = jnp.where(tier == 0, levels[1], jnp.where(tier == 1, levels[2], levels[3]))
            share = frac[lev]
            result = (1.0 - share) * low + share * high
            if lev:
                fs1[m, lev - 1] = result
            else:
                fs0[m] = result
                for k in range(TASKS):
                    right = result[:, 256 * (k + 1) % 1024 : 256 * (k + 1) % 1024 + 128]
                    left = result[:, (256 * k - 128) % 1024 : (256 * k - 128) % 1024 + 128]
                    rim = pltpu.roll(jnp.where(lane >= 124, left, right), m * 8 + 4, 1)
                    es[k] = jnp.where(lane // 8 == m, rim, es[k])
        return carry

    here_cols = pl.ds(pl.multiple_of(256 * t, 256), 256)
    local = []
    swaps = {}
    windows = {}

    def block(src, c):
        return pl.ds(pl.multiple_of(16 * src + 4 * c, 4), 4)

    def exchange(c):
        chunk = pl.ds(4 * c, 4)
        copy = pltpu.make_async_copy(
            fs0.at[chunk, :, here_cols], w5.at[2, block(t, c)], own.at[1 + c]
        )
        copy.start()
        local.append(copy)
        for k in (1, 2, 3):
            to = peer[k]
            cols = pl.ds(pl.multiple_of(256 * to, 256), 256)
            i = 3 * c + k - 1
            swaps[c, k] = send(
                fs0.at[chunk, :, cols], w5.at[2, block(t, c)], swap_s.at[i], swap_r.at[i], (to, s)
            )

    def forward(c):
        for k in range(TASKS):
            src = lax.rem(t - k + TASKS, TASKS)
            part = block(src, c)
            if k:
                swaps[c, k].wait_recv()
                held = w5.at[2, part]
            else:
                held = fs0.at[pl.ds(4 * c, 4), :, here_cols]
            for j, (to, slot) in enumerate(
                ((other, 2 + way), (second, 2 - 2 * way), (mate, 2 - way))
            ):
                i = 16 * j + 4 * c + k
                windows[j, c, k] = send(
                    held, w5.at[slot, part], win_s.at[i], win_r.at[i], (t, to)
                )

    def relay(c):
        for k in range(TASKS):
            src = lax.rem(t - k + TASKS, TASKS)
            part = block(src, c)
            windows[0, c, k].wait_recv()
            i = 48 + 4 * c + k
            windows[3, c, k] = send(
                w5.at[2 - way, part], w5.at[2 - 2 * way, part],
                win_s.at[i], win_r.at[i], (t, mate),
            )

    for c in range(4):
        halo_copies[2 * c].wait_recv()
        halo_copies[2 * c + 1].wait_recv()
        lax.fori_loop(4 * c, 4 * c + 4, member, 0)
        exchange(c)
        if c == 3:
            rims = []
            for k in (1, 2, 3):
                rims.append(
                    send(
                        es.at[peer[k]], e5.at[2, t], rim_s.at[k - 1], rim_r.at[k - 1], (peer[k], s)
                    )
                )
            own_rim = pltpu.make_async_copy(es.at[t], e5.at[2, t], own.at[5])
            own_rim.start()
        if c:
            forward(c - 1)
    forward(3)
    attr_copies = [
        send(attr, attr5.at[2 - d], attr_s.at[i], attr_r.at[i], (t, strip[d]))
        for i, d in enumerate((-2, -1, 1, 2))
    ]
    own_rim.wait()
    for copy in rims:
        copy.wait_recv()
    edges = [
        send(e5.at[2], e5.at[2 - d], edge_s.at[i], edge_r.at[i], (t, strip[d]))
        for i, d in enumerate((-2, -1, 1, 2))
    ]
    for c in range(4):
        relay(c)
    for copy in halo_copies + rims:
        copy.wait_send()
    for copy in swaps.values():
        copy.wait_send()
    for copy in local:
        copy.wait()
    for (j, c, k), copy in windows.items():
        copy.wait_send()
        if j:
            copy.wait_recv()
    for copy in attr_copies + edges:
        copy.wait()
    own_attr.wait()


def forecast(x, wet, donor, frac, rate, pos, value, var):
    dma = pltpu.SemaphoreType.DMA
    vmem = pl.BlockSpec(memory_space=pltpu.VMEM)
    anywhere = pl.BlockSpec(memory_space=pl.ANY)
    return pl.pallas_call(
        forecast_kernel,
        out_shape=[
            jax.ShapeDtypeStruct((5, 64, 8, 256), F32),
            jax.ShapeDtypeStruct((16, 3, 8, 1024), F32),
            jax.ShapeDtypeStruct((5, 4, 8, 128), F32),
            jax.ShapeDtypeStruct((5, 3, 32, 128), F32),
        ],
        in_specs=[vmem] * 4 + [pl.BlockSpec(memory_space=pltpu.SMEM)] + [vmem] * 3,
        out_specs=[anywhere, vmem, anywhere, anywhere],
        scratch_shapes=[
            pltpu.VMEM((16, 4, 8, 1024), F32),
            pltpu.VMEM((8, 1024), jnp.int32),
            pltpu.VMEM((16, 8, 1024), F32),
            pltpu.VMEM((4, 8, 128), F32),
            pltpu.VMEM((3, 32, 128), F32),
            dma((8,)), dma((8,)), dma((2,)), dma((2,)), dma((4,)), dma((4,)),
            dma((6,)), dma((12,)), dma((12,)), dma((3,)), dma((3,)),
            dma((64,)), dma((64,)), dma((4,)), dma((4,)),
        ],
        compiler_params=pltpu.CompilerParams(
            collective_id=0, has_side_effects=True, vmem_limit_bytes=LIMIT
        ),
    )(x, wet, donor, frac, rate, pos, value, var)


def spread(x, shift):
    lane = iota(x.shape, 1)
    return jnp.where(
        lane < 64, pltpu.roll(x, (127 - shift) % 128, 1), pltpu.roll(x, 63 - shift, 1)
    )


def beside(x):
    hi, lo = split(x)
    return jnp.concatenate([hi, lo], axis=1)


def doubled(both):
    left = jnp.where(iota((64, 128), 1) < 64, 1.0, 0.0)
    left, right = left.astype(BF16), (1.0 - left).astype(BF16)
    hi, lo = both[:, :128], both[:, 128:]
    hi = jnp.concatenate([hi * left, hi * right], axis=0)
    lo = jnp.concatenate([lo * left, lo * right], axis=0)
    return jnp.concatenate(
        [
            jnp.concatenate([hi, lo], axis=1),
            jnp.concatenate([hi, jnp.zeros((128, 128), BF16)], axis=1),
        ],
        axis=0,
    )


def times(both, weights):
    product = jnp.dot(both, weights, preferred_element_type=F32)
    return product[:, :128] + product[:, 128:]


def weights_kernel(
    w5, e5, attr, listed, live, fs1,
    every, f1,
    out, cols, rim, mean, picked, base, taper, force, system, drive,
    own, swap_s, swap_r, row_s, row_r, keep_s, side_s, side_r, corner_s, corner_r,
):
    t = lax.axis_index("task")
    s = lax.axis_index("patch")
    up, down = lax.rem(s + STRIPS - 1, STRIPS), lax.rem(s + 1, STRIPS)
    peer = {k: lax.rem(t + k, TASKS) for k in range(TASKS)}
    right, left = peer[1], peer[3]
    greet(
        [(peer[k], s) for k in (1, 2, 3)]
        + [(t, up), (t, down)]
        + [(x, y) for x in (right, left) for y in (up, down)]
    )
    mine = pl.ds(pl.multiple_of(16 * t, 16), 16)
    here_cols = pl.ds(pl.multiple_of(256 * t, 256), 256)
    own_copy = pltpu.make_async_copy(fs1.at[:, :, :, here_cols], f1.at[mine], own.at[0])
    own_copy.start()
    swaps = []
    for k in (1, 2, 3):
        to_cols = pl.ds(pl.multiple_of(256 * peer[k], 256), 256)
        copy = sender(
            fs1.at[:, :, :, to_cols], f1.at[mine], swap_s.at[k - 1], swap_r.at[k - 1], (peer[k], s)
        )
        copy.start()
        swaps.append(copy)

    def rows_of(n):
        part = pl.ds(n * (GROUP // 2), GROUP // 2)
        there = pl.ds(1 + n * (GROUP // 2), GROUP // 2)
        copies = []
        for a in range(2):
            copies.append(
                sender(
                    out.at[a, part], every.at[3 - 3 * a, there],
                    row_s.at[a, n], row_r.at[a, n], (t, (up, down)[a]),
                )
            )
            copies.append(
                pltpu.make_async_copy(out.at[a, part], every.at[1 + a, there], keep_s.at[a, n])
            )
        return copies

    lane = iota((8, 128), 1)
    sub = iota((8, 128), 0)

    def place(st, carry):
        for src in range(TASKS):
            tile = e5[st, src]
            for m in range(16):
                rim[16 * src + m] = pltpu.roll(tile, (128 - 8 * m) % 128, 1) if m else tile
        rows = pl.ds(pl.multiple_of(8 * st, 8), 8)
        means, rim_means = [], []
        for r in range(8):
            whole = w5[st, :, r, :]
            mu = jnp.sum(whole, axis=0, keepdims=True) * (1.0 / 64)
            dev = whole - mu
            cols[4:260, st, r, :] = jnp.concatenate([dev, dev], axis=0).T
            means.append(mu)
            whole = rim[:, r, :]
            mu = jnp.sum(whole, axis=0, keepdims=True) * (1.0 / 64)
            dev = whole - mu
            turned = jnp.concatenate([dev, dev], axis=0).T
            cols[0:4, st, r, :] = turned[0:4]
            cols[260:264, st, r, :] = turned[4:8]
            rim_means.append(mu)
        mean[rows, 0:256] = jnp.concatenate(means, axis=0)
        mean[rows, 256:384] = jnp.concatenate(rim_means, axis=0)
        return carry

    lax.fori_loop(0, 5, place, 0)

    spot = iota((384, 128), 0)
    coarse = iota((384, 128), 1)
    lane_of = iota((40, 384), 1)
    known = jnp.where(lane_of < 264, mean[...], 0.0)
    for q in range(4):
        want = jnp.where(
            coarse == 0, 256 + q, jnp.where(coarse == 65, 260 + q, 4 * coarse - 4 + q)
        )
        picked[q] = jnp.dot(
            known,
            jnp.where((spot == want) & (coarse < 66), 1.0, 0.0),
            precision=lax.Precision.HIGHEST,
            preferred_element_type=F32,
        )
    flat = listed[...]
    block_col = 4 * (iota((128, 32), 0) % 64) + 256 * t - 4
    code = ((flat // 8192 - (s - 2)) * 9 + flat % 8192 // 8 - block_col) * 8 + flat % 8
    code = code.astype(F32).T.astype(jnp.int32)
    pick = iota((64, 128), 0)
    into = iota((64, 128), 1)
    counts = live[...].astype(F32)
    alive = jnp.dot(
        counts, jnp.where(pick == into, 1.0, 0.0), preferred_element_type=F32
    )[0:1] + jnp.dot(counts, jnp.where(pick == into - 64, 1.0, 0.0), preferred_element_type=F32)[1:2]
    for slot in range(32):
        kept = jnp.where(alive > slot, code[slot : slot + 1, :], -100000)
        base[slot] = jnp.broadcast_to(kept, (8, 128)) - sub

    point_row = jnp.where(lane < 64, 1.5, 5.5)
    height = sub.astype(F32)
    taper[45] = jnp.zeros((8, 128), F32)

    def weigh(st, carry):
        for cr in range(9):
            q, shift = (cr - 4) % 4, (cr - 4) // 4
            row = spread(attr[st, 0, 8 * q : 8 * q + 8, :], shift)
            value = spread(attr[st, 1, 8 * q : 8 * q + 8, :], shift)
            var = spread(attr[st, 2, 8 * q : 8 * q + 8, :], shift)
            tile = (st * 9 + cr) * 8
            count = jnp.zeros((8, 128), F32)
            for slot in range(32):
                count = count + jnp.where(base[slot] == tile, 1.0, 0.0)
            apart = row + (8.0 * (st - 2).astype(F32)) - point_row
            dist = apart * apart + (cr - 5.5) ** 2
            weight = count * jnp.exp(dist * (-1.0 / 1152.0)) / var
            pull = weight * value
            total = jnp.zeros((8, 128), F32)
            pulled = jnp.zeros((8, 128), F32)
            for k in range(8):
                hit = row[k : k + 1] == height
                total = total + jnp.where(hit, weight[k : k + 1], 0.0)
                pulled = pulled + jnp.where(hit, pull[k : k + 1], 0.0)
            centre = spread(picked[q, pl.ds(pl.multiple_of(8 * st, 8), 8), :], shift)
            taper[cr * 5 + st] = total
            force[cr * 5 + st] = pulled - total * centre
        return carry

    lax.fori_loop(0, 5, weigh, 0)

    tall_lane = iota((368, 128), 1)
    eye = jnp.where(iota((64, 128), 0) == iota((64, 128), 1) % 64, 1.0, 0.0)

    def gram(b):
        index = jnp.where(lane < 64, b, 64 + b)
        near = cols[pl.ds(4 * b, 10)].reshape(400, 128)[:368]
        spread_taper = jnp.concatenate(
            [jnp.take_along_axis(taper[k], index, axis=1) for k in range(46)], axis=0
        )
        spread_force = jnp.concatenate(
            [jnp.take_along_axis(force[k], index, axis=1) for k in range(45)], axis=0
        )
        s_hi, s_lo = split(near * spread_taper)
        n_hi = near.astype(BF16).astype(F32)
        both = jnp.where(tall_lane < 64, n_hi, near - n_hi).astype(BF16)
        product = lax.dot_general(
            both,
            jnp.concatenate([s_hi, s_lo], axis=1),
            (((0,), (0,)), ((), ())),
            preferred_element_type=F32,
        )
        product = product[:64] + product[64:]
        return (
            product[:, :128] + product[:, 128:] + 63.0 * eye,
            jnp.sum(near[:360] * spread_force, axis=0, keepdims=True),
        )

    def keep(k, made):
        system[k] = made[0]
        drive[k] = jnp.broadcast_to(made[1], (8, 128))

    for k in range(GROUP):
        keep(k, gram(k))

    half = iota((64, 128), 1) < 64

    def solve(n, carry):
        nears, inverses, norms = [], [], []
        systems = [system[k] for k in range(GROUP)]
        drives = [drive[k][:1] for k in range(GROUP)]
        later = jnp.minimum(n + 1, 64 // GROUP - 1) * GROUP
        made = []

        def share(n):
            for k in range(n * GROUP // (2 * NS_ITERS), (n + 1) * GROUP // (2 * NS_ITERS)):
                made.append(gram(later + k))

        for x in systems:
            squares = jnp.sum(x * x, axis=0, keepdims=True)
            left = iota((1, 128), 1) < 64
            one = jnp.sum(jnp.where(left, squares, 0.0), axis=1, keepdims=True)
            two = jnp.sum(jnp.where(left, 0.0, squares), axis=1, keepdims=True)
            norm = jnp.sqrt(jnp.where(left, one, two))
            norms.append(norm)
            nears.append(x / norm)
            inverses.append(None)
        for turn in range(NS_ITERS):
            share(2 * turn)
            parts = [beside(x) for x in nears]
            weights = [doubled(x) for x in parts]
            if turn == 0:
                inverses = [1.5 * eye - 0.5 * x for x in nears]
                squared = [times(x, y) for x, y in zip(parts, weights)]
            elif turn < NS_ITERS - 1:
                squared = []
                for k in range(GROUP):
                    product = times(
                        jnp.concatenate([parts[k], beside(inverses[k])], axis=0), weights[k]
                    )
                    squared.append(product[:64])
                    inverses[k] = 1.5 * inverses[k] - 0.5 * product[64:]
            else:
                inverses = [
                    1.5 * x - 0.5 * times(beside(x), y) for x, y in zip(inverses, weights)
                ]
            share(2 * turn + 1)
            if turn < NS_ITERS - 1:
                nears = [
                    2.25 * x - 1.5 * y + 0.25 * times(beside(y), z)
                    for x, y, z in zip(nears, squared, weights)
                ]

        def standing(x):
            one = jnp.sum(jnp.where(half, x, 0.0), axis=1, keepdims=True)
            two = jnp.sum(jnp.where(half, 0.0, x), axis=1, keepdims=True)
            return jnp.where(half, one, two)

        finals = []
        for k in range(GROUP):
            z = inverses[k]
            once = jnp.sum(z * standing(eye * drives[k]), axis=0, keepdims=True)
            drift = standing(z * (once / norms[k]))
            finals.append(jnp.sqrt(63.0 / norms[k]) * z + drift)
        for k in range(0, GROUP, 2):
            g = n * (GROUP // 2) + k // 2
            out[0, g] = jnp.where(half, finals[k], pltpu.roll(finals[k + 1], 64, 1))
            out[1, g] = jnp.where(half, pltpu.roll(finals[k], 64, 1), finals[k + 1])
        for k in range(GROUP):
            keep(k, made[k])
        for copy in rows_of(n):
            copy.start()
        return carry

    lax.fori_loop(0, 64 // GROUP, solve, 0)

    sides = []
    for i, (to, at, there) in enumerate([(right, 31, 0), (left, 0, 33)]):
        for a in range(2):
            sides.append(
                sender(
                    out.at[a, at], every.at[1 + a, there],
                    side_s.at[2 * i + a], side_r.at[2 * i + a], (to, s),
                )
            )
            sides.append(
                sender(
                    out.at[a, at], every.at[3 - 3 * a, there],
                    corner_s.at[2 * i + a], corner_r.at[2 * i + a], (to, (up, down)[a]),
                )
            )
    for copy in sides:
        copy.start()

    def settle(n, carry):
        for copy in rows_of(n):
            copy.wait()
        return carry

    lax.fori_loop(0, 64 // GROUP, settle, 0)
    for copy in sides + swaps:
        copy.wait()
    own_copy.wait()


def point_weights(w5, e5, attr5, listed, live, fs1):
    dma = pltpu.SemaphoreType.DMA
    vmem = pl.BlockSpec(memory_space=pltpu.VMEM)
    anywhere = pl.BlockSpec(memory_space=pl.ANY)
    turns = 64 // GROUP
    return pl.pallas_call(
        weights_kernel,
        out_shape=[
            jax.ShapeDtypeStruct((4, 34, 64, 128), F32),
            jax.ShapeDtypeStruct((64, 3, 8, 256), F32),
        ],
        in_specs=[vmem] * 5 + [anywhere],
        out_specs=[anywhere] * 2,
        scratch_shapes=[
            pltpu.VMEM((2, 32, 64, 128), F32),
            pltpu.VMEM((264, 5, 8, 128), F32),
            pltpu.VMEM((64, 8, 128), F32),
            pltpu.VMEM((40, 384), F32),
            pltpu.VMEM((4, 40, 128), F32),
            pltpu.VMEM((32, 8, 128), jnp.int32),
            pltpu.VMEM((46, 8, 128), F32),
            pltpu.VMEM((45, 8, 128), F32),
            pltpu.VMEM((GROUP, 64, 128), F32),
            pltpu.VMEM((GROUP, 8, 128), F32),
            dma((1,)), dma((3,)), dma((3,)), dma((2, turns)), dma((2, turns)), dma((2, turns)),
            dma((4,)), dma((4,)), dma((4,)), dma((4,)),
        ],
        compiler_params=pltpu.CompilerParams(
            collective_id=2, has_side_effects=True, vmem_limit_bytes=LIMIT
        ),
    )(w5, e5, attr5, listed, live, fs1)


def hat(x):
    return jnp.maximum(1.0 - jnp.abs(x - 1.5) * 0.25, 0.0)


def analysis_kernel(
    every_in, w5, f1, wet,
    out,
    every, f0, turned, mid, top, low, total, result,
    own, back_s, back_r,
):
    t = lax.axis_index("task")
    s = lax.axis_index("patch")
    peer = {k: lax.rem(t + k, TASKS) for k in range(TASKS)}
    load = pltpu.make_async_copy(w5.at[2], f0, own.at[0])
    load.start()
    fetch = pltpu.make_async_copy(every_in, every, own.at[1])
    fetch.start()
    greet([(peer[k], s) for k in (1, 2, 3)])

    total[...] = jnp.zeros_like(total)
    load.wait()
    cols = pl.ds(pl.multiple_of(256 * t, 256), 256)

    def field(lev, r):
        return f0[:, r, :] if lev == 0 else f1[:, lev - 1, r, :]

    for lev in range(4):
        for r in range(8):
            whole = field(lev, r)
            dev = whole - jnp.sum(whole, axis=0, keepdims=True) * (1.0 / 64)
            turned[10:266, r // 2, 4 * (r % 2) + lev, :] = jnp.concatenate([dev, dev], axis=0).T

    lane = iota((8, 128), 1)
    row = iota((8, 128), 0) // 4
    second = jnp.where(lane < 64, 0.0, 4.0)
    first_strip = jnp.where(s == 0, 1.0, 0.0)
    last_strip = jnp.where(s == STRIPS - 1, 1.0, 0.0)

    def row_share(a, k):
        r = (2 * k + row).astype(F32)
        if a == -1:
            return hat(r + 4.0) * (1.0 - first_strip)
        if a == 0:
            return hat(r) + hat(r + 4.0) * first_strip
        if a == 1:
            return hat(r - 4.0) + hat(r - 8.0) * last_strip
        return hat(r - 8.0) * (1.0 - last_strip)

    left = iota((8, 8, 128), 2) < 64

    def parted(x, share):
        x = x * share[None]
        high = x.astype(BF16).astype(F32)
        return jnp.where(left, high, x - high)

    for ref in (mid, top, low):
        ref[...] = jnp.zeros_like(ref)

    def part(n, carry):
        for k, a, ref in ((0, -1, top), (3, 1, low)):
            x = turned[pl.ds(8 * n + 10, 8), k]
            both = jnp.concatenate(
                [parted(x, row_share(a, k)), parted(x, row_share(a + 1, k))], axis=2
            )
            ref[pl.ds(pl.multiple_of(64 * n + 80, 16), 64)] = both.reshape(64, 256).astype(BF16)
        pieces = []
        for k in (1, 2):
            x = turned[pl.ds(8 * n + 10, 8), k]
            pieces.append(
                jnp.concatenate([parted(x, row_share(0, k)), parted(x, row_share(1, k))], axis=2)
            )
        both = jnp.stack(pieces, axis=1)
        mid[pl.ds(pl.multiple_of(128 * n + 160, 16), 128)] = both.reshape(128, 256).astype(BF16)
        return carry

    lax.fori_loop(0, 32, part, 0)

    def col_share(g):
        first = jnp.where((g == 0) & (t == 0), 1.0, 0.0)
        last = jnp.where((g == 31) & (t == TASKS - 1), 1.0, 0.0)
        alive = jnp.where(
            ((g == -1) & (t == 0)) | ((g == 32) & (t == TASKS - 1)), 0.0, 1.0
        )
        shares = []
        for c in range(12):
            x = (c - 2.0) - second
            share = hat(x)
            if c in (2, 3):
                share = share + jnp.where(lane < 64, hat(x + 4.0), 0.0) * first
            if c in (8, 9):
                share = share + jnp.where(lane < 64, 0.0, hat(x - 4.0)) * last
            shares.append(share * alive)
        return shares

    def paired(x):
        hi, lo = split(x)
        zero = jnp.zeros((64, 128), BF16)
        return jnp.concatenate(
            [jnp.concatenate([hi, lo], axis=1), jnp.concatenate([hi, zero], axis=1)], axis=0
        )

    def blend(n, carry):
        g = n - 1
        shares = col_share(g)
        operands = [paired(every[a, n]) for a in range(4)]
        for a, ref, height, first in ((0, top, 8, 0), (1, mid, 16, 1), (2, low, 8, 3)):
            rows = ref[pl.ds(pl.multiple_of(height * (8 * g + 8), 16), 12 * height)]
            product = jnp.dot(
                rows,
                jnp.concatenate([operands[a], operands[a + 1]], axis=0),
                preferred_element_type=F32,
            )
            product = (product[:, :128] + product[:, 128:]).reshape(12, height // 8, 8, 128)
            for c in range(12):
                total[8 * g + 8 + c, first : first + height // 8] += product[c] * shares[c][None]
        return carry

    fetch.wait()
    mine = pl.ds(pl.multiple_of(16 * t, 16), 16)
    copies = []
    for h in range(2):
        if h == 0:
            lax.fori_loop(0, 18, blend, 0)
        else:
            lax.fori_loop(18, 34, blend, 0)
        here = slice(128 * h, 128 * h + 128)
        ocean_cols = pl.ds(pl.multiple_of(256 * t + 128 * h, 128), 128)
        for r in range(8):
            ocean = wet[r : r + 1, ocean_cols].astype(F32)
            for lev in range(4):
                back = total[10 + 128 * h : 138 + 128 * h, r // 2, 4 * (r % 2) + lev, :].T
                whole = field(lev, r)[:, here]
                dev = whole - jnp.sum(whole, axis=0, keepdims=True) * (1.0 / 64)
                result[:, lev, r, here] = whole + ocean * (back[:64] + back[64:] - dev)
        copy = pltpu.make_async_copy(
            result.at[mine, :, :, here], out.at[:, :, :, ocean_cols], own.at[2 + h]
        )
        copy.start()
        copies.append(copy)
        for k in (1, 2, 3):
            theirs = pl.ds(pl.multiple_of(16 * peer[k], 16), 16)
            copy = sender(
                result.at[theirs, :, :, here], out.at[:, :, :, ocean_cols],
                back_s.at[3 * h + k - 1], back_r.at[3 * h + k - 1], (peer[k], s),
            )
            copy.start()
            copies.append(copy)
    for copy in copies:
        copy.wait()


def analysed(every, w5, f1, wet):
    dma = pltpu.SemaphoreType.DMA
    vmem = pl.BlockSpec(memory_space=pltpu.VMEM)
    anywhere = pl.BlockSpec(memory_space=pl.ANY)
    return pl.pallas_call(
        analysis_kernel,
        out_shape=jax.ShapeDtypeStruct((16, 4, 8, 1024), F32),
        in_specs=[anywhere, anywhere, vmem, vmem],
        out_specs=anywhere,
        scratch_shapes=[
            pltpu.VMEM((4, 34, 64, 128), F32),
            pltpu.VMEM((64, 8, 256), F32),
            pltpu.VMEM((SPAN, 4, 8, 128), F32),
            pltpu.VMEM((SPAN * 16, 256), BF16),
            pltpu.VMEM((SPAN * 8, 256), BF16),
            pltpu.VMEM((SPAN * 8, 256), BF16),
            pltpu.VMEM((SPAN, 4, 8, 128), F32),
            pltpu.VMEM((64, 4, 8, 256), F32),
            dma((4,)), dma((6,)), dma((6,)),
        ],
        compiler_params=pltpu.CompilerParams(
            collective_id=1, has_side_effects=True, vmem_limit_bytes=LIMIT
        ),
    )(every, w5, f1, wet)


def body(
    trials_initial_dye,
    diffusivity,
    wet_mask,
    deeper_donor_tier,
    shallower_tier_fraction,
    obs_pos,
    obs_value,
    obs_var,
    observation_list,
    obs_count,
):
    w5, fs1, e5, attr5 = forecast(
        trials_initial_dye,
        wet_mask,
        deeper_donor_tier,
        shallower_tier_fraction,
        diffusivity,
        obs_pos.reshape(64, 128),
        obs_value.reshape(64, 128),
        obs_var.reshape(64, 128),
    )
    every, f1 = point_weights(
        w5, e5, attr5, observation_list.reshape(128, 32), obs_count, fs1
    )
    return analysed(every, w5, f1, wet_mask)


def solution(mesh):
    return jax.shard_map(
        body,
        mesh=mesh,
        in_specs=(
            P("task", None, "patch", None),
            P(),
            P("patch", None),
            P(None, "patch", None),
            P(None, "patch", None),
            P("patch"),
            P("patch"),
            P("patch"),
            P("patch", "task", None),
            P("patch", "task"),
        ),
        out_specs=P("task", None, "patch", None),
        check_vma=False,
    )
```

time: 188 us -> 132 us (0.70)
  Pallas kernels: 179 us -> 127 us
  local copies, waits for them, and re-layouts: 6.58 us -> 4.63 us
    pallas_call x1, Pallas kernels: 71 us -> 41.8 us  [point_weights(): pl.pallas_call(weights_kernel, out_shape=[jax.ShapeDtypeStruct((4, 34, 64...]
    pallas_call x1, Pallas kernels: 55.2 us -> 41 us  [analysed(): pl.pallas_call(analysis_kernel, out_shape=jax.ShapeDtypeStruct((16, 4, 8,...]
    pallas_call x1, Pallas kernels: 53.1 us -> 44.5 us  [forecast(): pl.pallas_call(forecast_kernel, out_shape=[jax.ShapeDtypeStruct((5, 64, 8...]
    another operation x6 -> x0, local copies, waits for them, and re-layouts: 1.99 us -> none  [body(): facts = jnp.stack([(obs_pos // 1024).astype(F32), obs_value, obs_var])]
    unnamed x1 -> x2, local copies, waits for them, and re-layouts: 3.16 us -> 4.63 us
where the time goes in v2:
time: 132 us
  Pallas kernels  127 us (96%)
  local copies, waits for them, and re-layouts  4.63 us (4%)
    pallas_call x1, Pallas kernels, forecast(): pl.pallas_call(forecast_kernel, out_shape=[jax.ShapeDtypeStruct((5, 64, 8...  44.5 us
    pallas_call x1, Pallas kernels, point_weights(): pl.pallas_call(weights_kernel, out_shape=[jax.ShapeDtypeStruct((4, 34, 64...  41.8 us
    pallas_call x1, Pallas kernels, analysed(): pl.pallas_call(analysis_kernel, out_shape=jax.ShapeDtypeStruct((16, 4, 8,...  41 us
    unnamed x2, local copies, waits for them, and re-layouts  4.63 us

profile of v2, /device:TPU:0, one launch (start us, length us, event | category | flops | bytes accessed | tf_op | source)
XLA Modules:
  0.0 131.9 jit_solution(5024716805435830704)
XLA Ops:
  0.0 1.5 %copy.11 = s32[2,64,32]{2,1,0:T(8,128)} copy(s32[2,64,32]{1,2,0:T(8,128)} %param.18) | data formatting | bytes 32768 | tf_op args[8]
  1.5 44.5 %shard_map.100 = (f32[5,64,8,256]{3,2,1,0:T(8,128)}, f32[16,3,8,1024]{3,2,1,0:T(8,128)}, f32[5,4,8,128]{3,2,1,0:T(8,128)}, f32[5,3,32,128]{3,2,1,0:T(8,128)}) custom-call(f32[16,4,8,1024]{3,2,1,0:T(8,128)} %x.1, s32[8,1024]{1,0:T(8,128)} %wet.3, s32[4,8,1024]{2,1,0:T(8,128)} %donor.1, f32[4,8,1024]{2,1,0:T(8,128)} %frac.1, f32[4]{0:T(128)} %rate.1, ...), custom_call_target="tpu_custom_call" | custom-call | tf_op jit(solution)/shard_map/pallas_call | solution.py:270
  46.0 41.8 %shard_map.101 = (f32[4,34,64,128]{3,2,1,0:T(8,128)}, f32[64,3,8,256]{3,2,1,0:T(8,128)}) custom-call(f32[5,64,8,256]{3,2,1,0:T(8,128)} %get-tuple-element.11.w5, f32[5,4,8,128]{3,2,1,0:T(8,128)} %get-tuple-element.12.e5, f32[5,3,32,128]{3,2,1,0:T(8,128)} %get-tuple-element.13.attr, s32[128,32]{1,0:T(8,128)} %bitcast.4, s32[2,64]{1,0:T(2,128)} %live.1, ...), custom_call_target="tpu_custom_call" | custom-call | tf_op jit(solution)/shard_map/pallas_call | solution.py:600
  87.8 41.0 %shard_map.102 = f32[16,4,8,1024]{3,2,1,0:T(8,128)} custom-call(f32[4,34,64,128]{3,2,1,0:T(8,128)} %get-tuple-element.15.every_in, f32[5,64,8,256]{3,2,1,0:T(8,128)} %get-tuple-element.11.w5, f32[64,3,8,256]{3,2,1,0:T(8,128)} %get-tuple-element.16.f1, s32[8,1024]{1,0:T(8,128)} %wet.3), custom_call_target="tpu_custom_call" | custom-call | tf_op jit(solution)/shard_map/pallas_call | solution.py:783
  128.7 3.2 %copy.13 = f32[16,4,8,1024]{3,2,1,0:T(8,128)} copy(f32[16,4,8,1024]{3,2,1,0:T(8,128)} %shard_map.102) | data formatting | bytes 4194304

commit v3 on v2

v3 whole, which is shorter than its diff:
```python
import functools

import jax
import jax.numpy as jnp
from jax import lax
from jax.experimental import pallas as pl
from jax.experimental.pallas import tpu as pltpu
from jax.sharding import PartitionSpec as P

MESH = pl.DeviceIdType.MESH
F32 = jnp.float32
BF16 = jnp.bfloat16
STEPS = 4
NS_ITERS = 6
TASKS = 4
STRIPS = 32
GROUP = 8
SPAN = 276
SOLVES = 64 // GROUP
LIMIT = 60 * 1024 * 1024


def iota(shape, dim):
    return lax.broadcasted_iota(jnp.int32, shape, dim)


def split(x):
    hi = x.astype(BF16)
    return hi, (x - hi.astype(F32)).astype(BF16)


def greet(peers):
    barrier = pltpu.get_barrier_semaphore()
    for peer in peers:
        pl.semaphore_signal(barrier, inc=1, device_id=peer, device_id_type=MESH)
    pl.semaphore_wait(barrier, len(peers))


def sender(src, dst, ss, rs, to):
    return pltpu.make_async_remote_copy(
        src_ref=src, dst_ref=dst, send_sem=ss, recv_sem=rs, device_id=to, device_id_type=MESH
    )


def spread(x, shift):
    lane = iota(x.shape, 1)
    return jnp.where(
        lane < 64, pltpu.roll(x, (127 - shift) % 128, 1), pltpu.roll(x, 63 - shift, 1)
    )


def beside(x):
    hi, lo = split(x)
    return jnp.concatenate([hi, lo], axis=1)


def doubled(both):
    left = jnp.where(iota((64, 128), 1) < 64, 1.0, 0.0)
    left, right = left.astype(BF16), (1.0 - left).astype(BF16)
    hi, lo = both[:, :128], both[:, 128:]
    hi = jnp.concatenate([hi * left, hi * right], axis=0)
    lo = jnp.concatenate([lo * left, lo * right], axis=0)
    return jnp.concatenate(
        [
            jnp.concatenate([hi, lo], axis=1),
            jnp.concatenate([hi, jnp.zeros((128, 128), BF16)], axis=1),
        ],
        axis=0,
    )


def times(both, weights):
    product = jnp.dot(both, weights, preferred_element_type=F32)
    return product[:, :128] + product[:, 128:]


def hat(x):
    return jnp.maximum(1.0 - jnp.abs(x - 1.5) * 0.25, 0.0)


def kernel(
    x, wet, donor, frac, rate, pos, value, var, listed, live,
    out,
    hal, whal, mixing, fs0, fs1, es, attr,
    w5, e5, attr5, f1,
    every, cols, rim, mean, picked, base, taper, force, system, drive,
    turned, mid, top, low, total, result,
    halo_s, halo_r, wet_s, wet_r, attr_s, attr_r, own, swap_s, swap_r, rim_s, rim_r,
    win_s, win_r, edge_s, edge_r,
    deep_s, deep_r, row_s, row_r, side_s, side_r, corner_s, corner_r, back_s, back_r,
):
    t = lax.axis_index("task")
    s = lax.axis_index("patch")
    strip = {d: lax.rem(s + d + STRIPS, STRIPS) for d in (-2, -1, 1, 2)}
    up, down = strip[-1], strip[1]
    peer = {k: lax.rem(t + k, TASKS) for k in range(TASKS)}
    beyond = ((peer[1], 31, 0), (peer[3], 0, 33))
    way = 1 - 2 * lax.rem(s, 2)
    mate = s + way
    second = lax.rem(s + 2 * way + STRIPS, STRIPS)
    other = lax.rem(s - way + STRIPS, STRIPS)
    greet(
        [(t, strip[d]) for d in (-2, -1, 1, 2)]
        + [(peer[k], s) for k in (1, 2, 3)]
        + [(peer[k], y) for k in (1, 3) for y in (up, down)]
    )

    def send(src, dst, ss, rs, to):
        copy = sender(src, dst, ss, rs, to)
        copy.start()
        return copy

    wet_copies = []
    halo_copies = []
    for i, d in enumerate((-1, 1)):
        part = pl.ds(4 * i, 4)
        wet_copies.append(
            send(wet.at[part], whal.at[part], wet_s.at[i], wet_r.at[i], (t, strip[d]))
        )
    for c in range(4):
        members = pl.ds(4 * c, 4)
        for i, d in enumerate((-1, 1)):
            part = pl.ds(4 * i, 4)
            halo_copies.append(
                send(
                    x.at[members, :, part],
                    hal.at[members, :, part],
                    halo_s.at[2 * c + i],
                    halo_r.at[2 * c + i],
                    (t, strip[d]),
                )
            )

    facts = jnp.concatenate(
        [(pos[...] // 1024).astype(F32).T, value[...].T, var[...].T], axis=0
    )
    spot = iota((64, 128), 0)
    coarse = iota((64, 128), 1) - 1
    gathered = jnp.zeros((96, 128), F32)
    for m in range(4):
        taken = (spot == (coarse + 4) // 4 - 1 + 16 * t) & ((coarse + 4) % 4 == m)
        rows = jnp.concatenate([facts[128 * i + 32 * m : 128 * i + 32 * m + 32] for i in range(3)])
        gathered = gathered + jnp.dot(
            rows,
            jnp.where(taken, 1.0, 0.0),
            precision=lax.Precision.HIGHEST,
            preferred_element_type=F32,
        )
    lane96 = iota((32, 128), 1)
    known = (lane96 - 1 + 64 * t >= 0) & (lane96 - 1 + 64 * t < 256)
    attr[0] = gathered[0:32]
    attr[1] = gathered[32:64]
    attr[2] = jnp.where(known, gathered[64:96], 1.0)
    attr_copies = [
        send(attr, attr5.at[2 - d], attr_s.at[i], attr_r.at[i], (t, strip[d]))
        for i, d in enumerate((-2, -1, 1, 2))
    ]
    own_attr = pltpu.make_async_copy(attr, attr5.at[2], own.at[0])
    own_attr.start()

    sub = iota((8, 128), 0)
    lane = iota((8, 128), 1)
    below = jnp.where(s < STRIPS - 1, 1.0, 0.0)
    above = jnp.where(s > 0, 1.0, 0.0)
    inside = jnp.where(sub < 4, below, above)
    for copy in wet_copies:
        copy.wait()
    ocean = wet[...].astype(F32)
    ocean_halo = whal[...].astype(F32) * jnp.where(iota((8, 1024), 0) < 4, below, above)
    for lev in range(4):
        for i, mask in enumerate((ocean, ocean_halo)):
            mixing[lev, i, 0] = mask * (1.0 - 4.0 * rate[lev])
            mixing[lev, i, 1] = mask * rate[lev]
    es[...] = jnp.zeros_like(es)

    def advance(x, y, lev, which):
        fresh = []
        east = [pltpu.roll(a, 127, 1) for a in x] + [jnp.zeros((8, 128), F32)]
        west = [jnp.zeros((8, 128), F32)] + [pltpu.roll(a, 1, 1) for a in x]
        for j in range(8):
            around = (
                jnp.where(sub == 7, pltpu.roll(y[j], 7, 0), pltpu.roll(x[j], 7, 0))
                + jnp.where(sub == 0, pltpu.roll(y[j], 1, 0), pltpu.roll(x[j], 1, 0))
                + jnp.where(lane == 127, east[j + 1], east[j])
                + jnp.where(lane == 0, west[j], west[j + 1])
            )
            here = slice(128 * j, 128 * j + 128)
            fresh.append(
                mixing[lev, which, 0, :, here] * x[j] + mixing[lev, which, 1, :, here] * around
            )
        return fresh

    def member(m, carry):
        levels = []
        for lev in range(4):
            here = [x[m, lev, :, 128 * j : 128 * j + 128] for j in range(8)]
            rest = [hal[m, lev, :, 128 * j : 128 * j + 128] * inside for j in range(8)]
            for step in range(STEPS):
                fresh = advance(here, rest, lev, 0)
                if step < STEPS - 1:
                    rest = advance(rest, here, lev, 1)
                here = fresh
            levels.append(here)
        surface = []
        for j in range(8):
            here = slice(128 * j, 128 * j + 128)
            for lev in range(4):
                tier = donor[lev, :, here]
                first, second = tier == 0, tier == 1
                one, two, three, four = (levels[i][j] for i in range(4))
                near = jnp.where(first, one, jnp.where(second, two, three))
                far = jnp.where(first, two, jnp.where(second, three, four))
                share = frac[lev, :, here]
                mixed = (1.0 - share) * near + share * far
                if lev:
                    fs1[m, lev - 1, :, here] = mixed
                else:
                    fs0[m, :, here] = mixed
                    surface.append(mixed)
        for k in range(TASKS):
            edge = jnp.where(lane >= 124, surface[(2 * k - 1) % 8], surface[(2 * k + 2) % 8])
            es[k] = jnp.where(lane // 8 == m, pltpu.roll(edge, m * 8 + 4, 1), es[k])
        return carry

    here_cols = pl.ds(pl.multiple_of(256 * t, 256), 256)
    local = []
    swaps = {}
    windows = {}

    def block(src, c):
        return pl.ds(pl.multiple_of(16 * src + 4 * c, 4), 4)

    def exchange(c):
        chunk = pl.ds(4 * c, 4)
        copy = pltpu.make_async_copy(
            fs0.at[chunk, :, here_cols], w5.at[2, block(t, c)], own.at[1 + c]
        )
        copy.start()
        local.append(copy)
        for k in (1, 2, 3):
            to = peer[k]
            cols = pl.ds(pl.multiple_of(256 * to, 256), 256)
            i = 3 * c + k - 1
            swaps[c, k] = send(
                fs0.at[chunk, :, cols], w5.at[2, block(t, c)], swap_s.at[i], swap_r.at[i], (to, s)
            )

    def forward(c):
        for k in range(TASKS):
            src = lax.rem(t - k + TASKS, TASKS)
            part = block(src, c)
            if k:
                swaps[c, k].wait_recv()
                held = w5.at[2, part]
            else:
                held = fs0.at[pl.ds(4 * c, 4), :, here_cols]
            for j, (to, slot) in enumerate(
                ((other, 2 + way), (second, 2 - 2 * way), (mate, 2 - way))
            ):
                i = 16 * j + 4 * c + k
                windows[j, c, k] = send(
                    held, w5.at[slot, part], win_s.at[i], win_r.at[i], (t, to)
                )

    def relay(c):
        for k in range(TASKS):
            src = lax.rem(t - k + TASKS, TASKS)
            part = block(src, c)
            windows[0, c, k].wait_recv()
            i = 48 + 4 * c + k
            windows[3, c, k] = send(
                w5.at[2 - way, part], w5.at[2 - 2 * way, part],
                win_s.at[i], win_r.at[i], (t, mate),
            )

    for c in range(4):
        halo_copies[2 * c].wait_recv()
        halo_copies[2 * c + 1].wait_recv()
        lax.fori_loop(4 * c, 4 * c + 4, member, 0)
        exchange(c)
        if c == 3:
            rims = []
            for k in (1, 2, 3):
                rims.append(
                    send(
                        es.at[peer[k]], e5.at[2, t], rim_s.at[k - 1], rim_r.at[k - 1], (peer[k], s)
                    )
                )
            own_rim = pltpu.make_async_copy(es.at[t], e5.at[2, t], own.at[5])
            own_rim.start()
        if c:
            forward(c - 1)
    forward(3)
    own_rim.wait()
    for copy in rims:
        copy.wait_recv()
    edges = [
        send(e5.at[2], e5.at[2 - d], edge_s.at[i], edge_r.at[i], (t, strip[d]))
        for i, d in enumerate((-2, -1, 1, 2))
    ]
    mine = pl.ds(pl.multiple_of(16 * t, 16), 16)
    own_deep = pltpu.make_async_copy(fs1.at[:, :, :, here_cols], f1.at[mine], own.at[6])
    own_deep.start()
    deeps = []
    for k in (1, 2, 3):
        to_cols = pl.ds(pl.multiple_of(256 * peer[k], 256), 256)
        deeps.append(
            send(
                fs1.at[:, :, :, to_cols], f1.at[mine],
                deep_s.at[k - 1], deep_r.at[k - 1], (peer[k], s),
            )
        )

    def place(st):
        for src in range(TASKS):
            tile = e5[st, src]
            for m in range(16):
                rim[16 * src + m] = pltpu.roll(tile, (128 - 8 * m) % 128, 1) if m else tile
        rows = pl.ds(pl.multiple_of(8 * st, 8), 8)
        means, rim_means = [], []
        for r in range(8):
            whole = w5[st, :, r, :]
            mu = jnp.sum(whole, axis=0, keepdims=True) * (1.0 / 64)
            dev = whole - mu
            cols[4:260, st, r, :] = jnp.concatenate([dev, dev], axis=0).T
            means.append(mu)
            whole = rim[:, r, :]
            mu = jnp.sum(whole, axis=0, keepdims=True) * (1.0 / 64)
            dev = whole - mu
            turned = jnp.concatenate([dev, dev], axis=0).T
            cols[0:4, st, r, :] = turned[0:4]
            cols[260:264, st, r, :] = turned[4:8]
            rim_means.append(mu)
        mean[rows, 0:256] = jnp.concatenate(means, axis=0)
        mean[rows, 256:384] = jnp.concatenate(rim_means, axis=0)

    for copy in local:
        copy.wait()
    place(2)
    flat = listed[...]
    block_col = 4 * (iota((128, 32), 0) % 64) + 256 * t - 4
    code = ((flat // 8192 - (s - 2)) * 9 + flat % 8192 // 8 - block_col) * 8 + flat % 8
    code = code.astype(F32).T.astype(jnp.int32)
    pick = iota((64, 128), 0)
    into = iota((64, 128), 1)
    counts = live[...].astype(F32)
    alive = jnp.dot(
        counts, jnp.where(pick == into, 1.0, 0.0), preferred_element_type=F32
    )[0:1] + jnp.dot(counts, jnp.where(pick == into - 64, 1.0, 0.0), preferred_element_type=F32)[1:2]
    for slot in range(32):
        kept = jnp.where(alive > slot, code[slot : slot + 1, :], -100000)
        base[slot] = jnp.broadcast_to(kept, (8, 128)) - sub

    for copy in attr_copies:
        copy.wait()
    own_attr.wait()
    point_row = jnp.where(lane < 64, 1.5, 5.5)
    height = sub.astype(F32)
    taper[45] = jnp.zeros((8, 128), F32)

    def weigh(st, carry):
        for cr in range(9):
            q, shift = (cr - 4) % 4, (cr - 4) // 4
            row = spread(attr5[st, 0, 8 * q : 8 * q + 8, :], shift)
            value = spread(attr5[st, 1, 8 * q : 8 * q + 8, :], shift)
            var = spread(attr5[st, 2, 8 * q : 8 * q + 8, :], shift)
            tile = (st * 9 + cr) * 8
            count = jnp.zeros((8, 128), F32)
            for slot in range(32):
                count = count + jnp.where(base[slot] == tile, 1.0, 0.0)
            apart = row + (8.0 * (st - 2).astype(F32)) - point_row
            dist = apart * apart + (cr - 5.5) ** 2
            weight = count * jnp.exp(dist * (-1.0 / 1152.0)) / var
            pull = weight * value
            held = jnp.zeros((8, 128), F32)
            pulled = jnp.zeros((8, 128), F32)
            for k in range(8):
                hit = row[k : k + 1] == height
                held = held + jnp.where(hit, weight[k : k + 1], 0.0)
                pulled = pulled + jnp.where(hit, pull[k : k + 1], 0.0)
            taper[cr * 5 + st] = held
            force[cr * 5 + st] = pulled
        return carry

    lax.fori_loop(0, 5, weigh, 0)

    def field(lev, r):
        return w5[2, :, r, :] if lev == 0 else f1[:, lev - 1, r, :]

    def turn(lev):
        for r in range(8):
            whole = field(lev, r)
            dev = whole - jnp.sum(whole, axis=0, keepdims=True) * (1.0 / 64)
            turned[10:266, r // 2, 4 * (r % 2) + lev, :] = jnp.concatenate([dev, dev], axis=0).T

    total[...] = jnp.zeros_like(total)
    for ref in (mid, top, low):
        ref[...] = jnp.zeros_like(ref)
    turn(0)

    for c in range(4):
        relay(c)
    for copy in edges:
        copy.wait()
    for j, slot in ((2, 2 + way), (0, 2 - way), (1, 2 - 2 * way), (3, 2 + 2 * way)):
        if j:
            for c in range(4):
                for k in range(TASKS):
                    windows[j, c, k].wait_recv()
        place(slot)

    spot = iota((384, 128), 0)
    coarse = iota((384, 128), 1)
    lane_of = iota((40, 384), 1)
    known = jnp.where(lane_of < 264, mean[...], 0.0)
    for q in range(4):
        want = jnp.where(
            coarse == 0, 256 + q, jnp.where(coarse == 65, 260 + q, 4 * coarse - 4 + q)
        )
        picked[q] = jnp.dot(
            known,
            jnp.where((spot == want) & (coarse < 66), 1.0, 0.0),
            precision=lax.Precision.HIGHEST,
            preferred_element_type=F32,
        )
    def recentre(st, carry):
        for cr in range(9):
            q, shift = (cr - 4) % 4, (cr - 4) // 4
            centre = spread(picked[q, pl.ds(pl.multiple_of(8 * st, 8), 8), :], shift)
            force[cr * 5 + st] = force[cr * 5 + st] - taper[cr * 5 + st] * centre
        return carry

    lax.fori_loop(0, 5, recentre, 0)

    tall_lane = iota((368, 128), 1)
    eye = jnp.where(iota((64, 128), 0) == iota((64, 128), 1) % 64, 1.0, 0.0)

    def gram(b):
        index = jnp.where(lane < 64, b, 64 + b)
        near = cols[pl.ds(4 * b, 10)].reshape(400, 128)[:368]
        spread_taper = jnp.concatenate(
            [jnp.take_along_axis(taper[k], index, axis=1) for k in range(46)], axis=0
        )
        spread_force = jnp.concatenate(
            [jnp.take_along_axis(force[k], index, axis=1) for k in range(45)], axis=0
        )
        s_hi, s_lo = split(near * spread_taper)
        n_hi = near.astype(BF16).astype(F32)
        both = jnp.where(tall_lane < 64, n_hi, near - n_hi).astype(BF16)
        product = lax.dot_general(
            both,
            jnp.concatenate([s_hi, s_lo], axis=1),
            (((0,), (0,)), ((), ())),
            preferred_element_type=F32,
        )
        product = product[:64] + product[64:]
        return (
            product[:, :128] + product[:, 128:] + 63.0 * eye,
            jnp.sum(near[:360] * spread_force, axis=0, keepdims=True),
        )

    def keep(k, made):
        system[k] = made[0]
        drive[k] = jnp.broadcast_to(made[1], (8, 128))

    for k in range(GROUP):
        keep(k, gram(64 - GROUP + k))

    half = iota((64, 128), 1) < 64

    def rows_of(i):
        n = lax.rem(i + SOLVES - 1, SOLVES)
        part = pl.ds(1 + n * (GROUP // 2), GROUP // 2)
        return [
            sender(
                every.at[1 + a, part], every.at[3 - 3 * a, part],
                row_s.at[a, i], row_r.at[a, i], (t, (up, down)[a]),
            )
            for a in range(2)
        ]

    def sides_of():
        copies = []
        for i, (to, at, there) in enumerate(beyond):
            for a in range(2):
                copies.append(
                    sender(
                        every.at[1 + a, at + 1], every.at[1 + a, there],
                        side_s.at[2 * i + a], side_r.at[2 * i + a], (to, s),
                    )
                )
                copies.append(
                    sender(
                        every.at[1 + a, at + 1], every.at[3 - 3 * a, there],
                        corner_s.at[2 * i + a], corner_r.at[2 * i + a], (to, (up, down)[a]),
                    )
                )
        return copies

    def solve(i, carry):
        n = lax.rem(i + SOLVES - 1, SOLVES)
        nears, inverses, norms = [], [], []
        systems = [system[k] for k in range(GROUP)]
        drives = [drive[k][:1] for k in range(GROUP)]
        later = jnp.minimum(i, SOLVES - 2) * GROUP
        made = []

        def share(n):
            for k in range(n * GROUP // (2 * NS_ITERS), (n + 1) * GROUP // (2 * NS_ITERS)):
                made.append(gram(later + k))

        for x in systems:
            squares = jnp.sum(x * x, axis=0, keepdims=True)
            left = iota((1, 128), 1) < 64
            one = jnp.sum(jnp.where(left, squares, 0.0), axis=1, keepdims=True)
            two = jnp.sum(jnp.where(left, 0.0, squares), axis=1, keepdims=True)
            norm = jnp.sqrt(jnp.where(left, one, two))
            norms.append(norm)
            nears.append(x / norm)
            inverses.append(None)
        for turn in range(NS_ITERS):
            share(2 * turn)
            parts = [beside(x) for x in nears]
            weights = [doubled(x) for x in parts]
            if turn == 0:
                inverses = [1.5 * eye - 0.5 * x for x in nears]
                squared = [times(x, y) for x, y in zip(parts, weights)]
            elif turn < NS_ITERS - 1:
                squared = []
                for k in range(GROUP):
                    product = times(
                        jnp.concatenate([parts[k], beside(inverses[k])], axis=0), weights[k]
                    )
                    squared.append(product[:64])
                    inverses[k] = 1.5 * inverses[k] - 0.5 * product[64:]
            else:
                inverses = [
                    1.5 * x - 0.5 * times(beside(x), y) for x, y in zip(inverses, weights)
                ]
            share(2 * turn + 1)
            if turn < NS_ITERS - 1:
                nears = [
                    2.25 * x - 1.5 * y + 0.25 * times(beside(y), z)
                    for x, y, z in zip(nears, squared, weights)
                ]

        def standing(x):
            one = jnp.sum(jnp.where(half, x, 0.0), axis=1, keepdims=True)
            two = jnp.sum(jnp.where(half, 0.0, x), axis=1, keepdims=True)
            return jnp.where(half, one, two)

        finals = []
        for k in range(GROUP):
            z = inverses[k]
            once = jnp.sum(z * standing(eye * drives[k]), axis=0, keepdims=True)
            drift = standing(z * (once / norms[k]))
            finals.append(jnp.sqrt(63.0 / norms[k]) * z + drift)
        for k in range(0, GROUP, 2):
            g = n * (GROUP // 2) + k // 2
            every[1, g + 1] = jnp.where(half, finals[k], pltpu.roll(finals[k + 1], 64, 1))
            every[2, g + 1] = jnp.where(half, pltpu.roll(finals[k], 64, 1), finals[k + 1])
        for k in range(GROUP):
            keep(k, made[k])
        for copy in rows_of(i):
            copy.start()

        @pl.when(i == 1)
        def _():
            for copy in sides_of():
                copy.start()

        return carry

    row = iota((8, 128), 0) // 4
    offset = jnp.where(lane < 64, 0.0, 4.0)
    first_strip = jnp.where(s == 0, 1.0, 0.0)
    last_strip = jnp.where(s == STRIPS - 1, 1.0, 0.0)

    def row_share(a, k):
        r = (2 * k + row).astype(F32)
        if a == -1:
            return hat(r + 4.0) * (1.0 - first_strip)
        if a == 0:
            return hat(r) + hat(r + 4.0) * first_strip
        if a == 1:
            return hat(r - 4.0) + hat(r - 8.0) * last_strip
        return hat(r - 8.0) * (1.0 - last_strip)

    left = iota((8, 8, 128), 2) < 64

    def parted(x, share):
        x = x * share[None]
        high = x.astype(BF16).astype(F32)
        return jnp.where(left, high, x - high)

    def part(n, carry):
        for k, a, ref in ((0, -1, top), (3, 1, low)):
            x = turned[pl.ds(8 * n + 10, 8), k]
            both = jnp.concatenate(
                [parted(x, row_share(a, k)), parted(x, row_share(a + 1, k))], axis=2
            )
            ref[pl.ds(pl.multiple_of(64 * n + 80, 16), 64)] = both.reshape(64, 256).astype(BF16)
        pieces = []
        for k in (1, 2):
            x = turned[pl.ds(8 * n + 10, 8), k]
            pieces.append(
                jnp.concatenate([parted(x, row_share(0, k)), parted(x, row_share(1, k))], axis=2)
            )
        both = jnp.stack(pieces, axis=1)
        mid[pl.ds(pl.multiple_of(128 * n + 160, 16), 128)] = both.reshape(128, 256).astype(BF16)
        return carry

    def col_share(g):
        first = jnp.where((g == 0) & (t == 0), 1.0, 0.0)
        last = jnp.where((g == 31) & (t == TASKS - 1), 1.0, 0.0)
        alive = jnp.where(
            ((g == -1) & (t == 0)) | ((g == 32) & (t == TASKS - 1)), 0.0, 1.0
        )
        shares = []
        for c in range(12):
            x = (c - 2.0) - offset
            share = hat(x)
            if c in (2, 3):
                share = share + jnp.where(lane < 64, hat(x + 4.0), 0.0) * first
            if c in (8, 9):
                share = share + jnp.where(lane < 64, 0.0, hat(x - 4.0)) * last
            shares.append(share * alive)
        return shares

    def paired(x):
        hi, lo = split(x)
        zero = jnp.zeros((64, 128), BF16)
        return jnp.concatenate(
            [jnp.concatenate([hi, lo], axis=1), jnp.concatenate([hi, zero], axis=1)], axis=0
        )

    def blend(n, carry):
        g = n - 1
        shares = col_share(g)
        operands = [paired(every[a, n]) for a in range(4)]
        for a, ref, height, first in ((0, top, 8, 0), (1, mid, 16, 1), (2, low, 8, 3)):
            rows = ref[pl.ds(pl.multiple_of(height * (8 * g + 8), 16), 12 * height)]
            product = jnp.dot(
                rows,
                jnp.concatenate([operands[a], operands[a + 1]], axis=0),
                preferred_element_type=F32,
            )
            product = (product[:, :128] + product[:, 128:]).reshape(12, height // 8, 8, 128)
            for c in range(12):
                total[8 * g + 8 + c, first : first + height // 8] += product[c] * shares[c][None]
        return carry

    def finish(h):
        copies = []
        here = slice(128 * h, 128 * h + 128)
        ocean_cols = pl.ds(pl.multiple_of(256 * t + 128 * h, 128), 128)
        for r in range(8):
            ocean = wet[r : r + 1, ocean_cols].astype(F32)
            for lev in range(4):
                back = total[10 + 128 * h : 138 + 128 * h, r // 2, 4 * (r % 2) + lev, :].T
                whole = field(lev, r)[:, here]
                dev = whole - jnp.sum(whole, axis=0, keepdims=True) * (1.0 / 64)
                result[:, lev, r, here] = whole + ocean * (back[:64] + back[64:] - dev)
        copy = pltpu.make_async_copy(
            result.at[mine, :, :, here], out.at[:, :, :, ocean_cols], own.at[7 + h]
        )
        copy.start()
        copies.append(copy)
        for k in (1, 2, 3):
            theirs = pl.ds(pl.multiple_of(16 * peer[k], 16), 16)
            copies.append(
                send(
                    result.at[theirs, :, :, here], out.at[:, :, :, ocean_cols],
                    back_s.at[3 * h + k - 1], back_r.at[3 * h + k - 1], (peer[k], s),
                )
            )
        return copies

    lax.fori_loop(0, SOLVES - 1, solve, 0)

    own_deep.wait()
    for copy in deeps:
        copy.wait_recv()
    for lev in (1, 2, 3):
        turn(lev)
    lax.fori_loop(0, 32, part, 0)

    def arrived(i, carry):
        for copy in rows_of(i):
            copy.wait_recv()
        return carry

    sides = sides_of()
    lax.fori_loop(0, SOLVES - 2, arrived, 0)
    for copy in sides:
        copy.wait_recv()
    lax.fori_loop(0, 18, blend, 0)
    copies = finish(0)
    lax.fori_loop(SOLVES - 1, SOLVES, solve, 0)
    lax.fori_loop(SOLVES - 2, SOLVES, arrived, 0)
    lax.fori_loop(18, 34, blend, 0)
    copies += finish(1)

    def departed(i, carry):
        for copy in rows_of(i):
            copy.wait_send()
        return carry

    lax.fori_loop(0, SOLVES, departed, 0)
    for copy in sides + deeps + halo_copies + rims:
        copy.wait_send()
    for copy in swaps.values():
        copy.wait_send()
    for copy in windows.values():
        copy.wait_send()
    for copy in copies:
        copy.wait()


def assimilate(*arrays):
    dma = pltpu.SemaphoreType.DMA
    vmem = pl.BlockSpec(memory_space=pltpu.VMEM)
    return pl.pallas_call(
        kernel,
        out_shape=jax.ShapeDtypeStruct((16, 4, 8, 1024), F32),
        in_specs=[vmem] * 4 + [pl.BlockSpec(memory_space=pltpu.SMEM)] + [vmem] * 5,
        out_specs=pl.BlockSpec(memory_space=pl.ANY),
        scratch_shapes=[
            pltpu.VMEM((16, 4, 8, 1024), F32),
            pltpu.VMEM((8, 1024), jnp.int32),
            pltpu.VMEM((4, 2, 2, 8, 1024), F32),
            pltpu.VMEM((16, 8, 1024), F32),
            pltpu.VMEM((16, 3, 8, 1024), F32),
            pltpu.VMEM((4, 8, 128), F32),
            pltpu.VMEM((3, 32, 128), F32),
            pltpu.VMEM((5, 64, 8, 256), F32),
            pltpu.VMEM((5, 4, 8, 128), F32),
            pltpu.VMEM((5, 3, 32, 128), F32),
            pltpu.VMEM((64, 3, 8, 256), F32),
            pltpu.VMEM((4, 34, 64, 128), F32),
            pltpu.VMEM((264, 5, 8, 128), F32),
            pltpu.VMEM((64, 8, 128), F32),
            pltpu.VMEM((40, 384), F32),
            pltpu.VMEM((4, 40, 128), F32),
            pltpu.VMEM((32, 8, 128), jnp.int32),
            pltpu.VMEM((46, 8, 128), F32),
            pltpu.VMEM((45, 8, 128), F32),
            pltpu.VMEM((GROUP, 64, 128), F32),
            pltpu.VMEM((GROUP, 8, 128), F32),
            pltpu.VMEM((SPAN, 4, 8, 128), F32),
            pltpu.VMEM((SPAN * 16, 256), BF16),
            pltpu.VMEM((SPAN * 8, 256), BF16),
            pltpu.VMEM((SPAN * 8, 256), BF16),
            pltpu.VMEM((SPAN, 4, 8, 128), F32),
            pltpu.VMEM((64, 4, 8, 256), F32),
            dma((8,)), dma((8,)), dma((2,)), dma((2,)), dma((4,)), dma((4,)),
            dma((9,)), dma((12,)), dma((12,)), dma((3,)), dma((3,)),
            dma((64,)), dma((64,)), dma((4,)), dma((4,)),
            dma((3,)), dma((3,)), dma((2, SOLVES)), dma((2, SOLVES)),
            dma((4,)), dma((4,)), dma((4,)), dma((4,)), dma((6,)), dma((6,)),
        ],
        compiler_params=pltpu.CompilerParams(
            collective_id=0, has_side_effects=True, vmem_limit_bytes=LIMIT
        ),
    )(*arrays)


def body(
    trials_initial_dye,
    diffusivity,
    wet_mask,
    deeper_donor_tier,
    shallower_tier_fraction,
    obs_pos,
    obs_value,
    obs_var,
    observation_list,
    obs_count,
):
    return assimilate(
        trials_initial_dye,
        wet_mask,
        deeper_donor_tier,
        shallower_tier_fraction,
        diffusivity,
        obs_pos.reshape(64, 128),
        obs_value.reshape(64, 128),
        obs_var.reshape(64, 128),
        observation_list.reshape(128, 32),
        obs_count,
    )


def solution(mesh):
    return jax.shard_map(
        body,
        mesh=mesh,
        in_specs=(
            P("task", None, "patch", None),
            P(),
            P("patch", None),
            P(None, "patch", None),
            P(None, "patch", None),
            P("patch"),
            P("patch"),
            P("patch"),
            P("patch", "task", None),
            P("patch", "task"),
        ),
        out_specs=P("task", None, "patch", None),
        check_vma=False,
    )
```

time: 132 us -> 116 us (0.88)
  Pallas kernels: 127 us -> 111 us
    pallas_call x3 -> x1, Pallas kernels: 127 us -> 111 us  [assimilate(): pl.pallas_call(kernel, out_shape=jax.ShapeDtypeStruct((16, 4, 8, 1024), F...]
where the time goes in v3:
time: 116 us; the launch traced here: 115 us
  Pallas kernels  111 us (96%)
  local copies, waits for them, and re-layouts  4.63 us (4%)
    pallas_call x1, Pallas kernels, assimilate(): pl.pallas_call(kernel, out_shape=jax.ShapeDtypeStruct((16, 4, 8, 1024), F...  111 us
    unnamed x2, local copies, waits for them, and re-layouts  4.63 us

profile of v3, /device:TPU:0, one launch (start us, length us, event | category | flops | bytes accessed | tf_op | source)
XLA Modules:
  0.0 115.4 jit_solution(15783237976310077215)
XLA Ops:
  0.0 1.5 %copy.11 = s32[2,64,32]{2,1,0:T(8,128)} copy(s32[2,64,32]{1,2,0:T(8,128)} %param.18) | data formatting | bytes 32768 | tf_op args[8]
  1.5 110.7 %shard_map.100 = f32[16,4,8,1024]{3,2,1,0:T(8,128)} custom-call(f32[16,4,8,1024]{3,2,1,0:T(8,128)} %x.1, s32[8,1024]{1,0:T(8,128)} %wet.1, s32[4,8,1024]{2,1,0:T(8,128)} %donor.1, f32[4,8,1024]{2,1,0:T(8,128)} %frac.1, f32[4]{0:T(128)} %rate.1, s32[64,128]{1,0:T(8,128)} %bitcast.5, f32[64,128]{1,0:T(8,128)} %bitcast.6, f32[64,128]{1,0:T(8,128)} %bitcast.7, ...), custom_call_target="tpu_custom_call" | custom-call | tf_op jit(solution)/shard_map/pallas_call | solution.py:723
  112.2 3.2 %copy.13 = f32[16,4,8,1024]{3,2,1,0:T(8,128)} copy(f32[16,4,8,1024]{3,2,1,0:T(8,128)} %shard_map.100) | data formatting | bytes 4194304

commit v4 on v3

--- a/solution.py
+++ b/solution.py
@@ -81,7 +81,7 @@
 def kernel(
     x, wet, donor, frac, rate, pos, value, var, listed, live,
     out,
-    hal, whal, mixing, fs0, fs1, es, attr,
+    hal, whal, mixing, ring, fs0, fs1, es, attr,
     w5, e5, attr5, f1,
     every, cols, rim, mean, picked, base, taper, force, system, drive,
     turned, mid, top, low, total, result,
@@ -173,14 +173,14 @@
             mixing[lev, i, 1] = mask * rate[lev]
     es[...] = jnp.zeros_like(es)
 
-    def advance(x, y, lev, which):
+    def advance(x, lev, which, row):
         fresh = []
         east = [pltpu.roll(a, 127, 1) for a in x] + [jnp.zeros((8, 128), F32)]
         west = [jnp.zeros((8, 128), F32)] + [pltpu.roll(a, 1, 1) for a in x]
         for j in range(8):
             around = (
-                jnp.where(sub == 7, pltpu.roll(y[j], 7, 0), pltpu.roll(x[j], 7, 0))
-                + jnp.where(sub == 0, pltpu.roll(y[j], 1, 0), pltpu.roll(x[j], 1, 0))
+                ring[lev, j, row + 1 : row + 9, :]
+                + ring[lev, j, row - 1 : row + 7, :]
                 + jnp.where(lane == 127, east[j + 1], east[j])
                 + jnp.where(lane == 0, west[j], west[j + 1])
             )
@@ -191,16 +191,24 @@
         return fresh
 
     def member(m, carry):
-        levels = []
-        for lev in range(4):
-            here = [x[m, lev, :, 128 * j : 128 * j + 128] for j in range(8)]
-            rest = [hal[m, lev, :, 128 * j : 128 * j + 128] * inside for j in range(8)]
-            for step in range(STEPS):
-                fresh = advance(here, rest, lev, 0)
+        levels = [
+            [x[m, lev, :, 128 * j : 128 * j + 128] for j in range(8)] for lev in range(4)
+        ]
+        rests = [
+            [hal[m, lev, :, 128 * j : 128 * j + 128] * inside for j in range(8)]
+            for lev in range(4)
+        ]
+        for step in range(STEPS):
+            for lev in range(4):
+                for j in range(8):
+                    ring[lev, j, 0:8, :] = rests[lev][j]
+                    ring[lev, j, 8:16, :] = levels[lev][j]
+                    ring[lev, j, 16:24, :] = rests[lev][j]
+                    ring[lev, j, 24:32, :] = levels[lev][j]
+            for lev in range(4):
+                levels[lev] = advance(levels[lev], lev, 0, 8)
                 if step < STEPS - 1:
-                    rest = advance(rest, here, lev, 1)
-                here = fresh
-            levels.append(here)
+                    rests[lev] = advance(rests[lev], lev, 1, 16)
         surface = []
         for j in range(8):
             here = slice(128 * j, 128 * j + 128)
@@ -223,7 +231,7 @@
         return carry
 
     here_cols = pl.ds(pl.multiple_of(256 * t, 256), 256)
-    local = []
+    local, own_deeps, deeps = [], [], []
     swaps = {}
     windows = {}
 
@@ -243,6 +251,21 @@
             i = 3 * c + k - 1
             swaps[c, k] = send(
                 fs0.at[chunk, :, cols], w5.at[2, block(t, c)], swap_s.at[i], swap_r.at[i], (to, s)
+            )
+        copy = pltpu.make_async_copy(
+            fs1.at[chunk, :, :, here_cols], f1.at[block(t, c)], own.at[9 + c]
+        )
+        copy.start()
+        own_deeps.append(copy)
+        for k in (1, 2, 3):
+            to = peer[k]
+            cols = pl.ds(pl.multiple_of(256 * to, 256), 256)
+            i = 3 * c + k - 1
+            deeps.append(
+                send(
+                    fs1.at[chunk, :, :, cols], f1.at[block(t, c)],
+                    deep_s.at[i], deep_r.at[i], (to, s),
+                )
             )
 
     def forward(c):
@@ -299,17 +322,6 @@
         for i, d in enumerate((-2, -1, 1, 2))
     ]
     mine = pl.ds(pl.multiple_of(16 * t, 16), 16)
-    own_deep = pltpu.make_async_copy(fs1.at[:, :, :, here_cols], f1.at[mine], own.at[6])
-    own_deep.start()
-    deeps = []
-    for k in (1, 2, 3):
-        to_cols = pl.ds(pl.multiple_of(256 * peer[k], 256), 256)
-        deeps.append(
-            send(
-                fs1.at[:, :, :, to_cols], f1.at[mine],
-                deep_s.at[k - 1], deep_r.at[k - 1], (peer[k], s),
-            )
-        )
 
     def place(st):
         for src in range(TASKS):
@@ -337,10 +349,9 @@
     for copy in local:
         copy.wait()
     place(2)
-    flat = listed[...]
-    block_col = 4 * (iota((128, 32), 0) % 64) + 256 * t - 4
+    flat = jnp.concatenate([listed[0], listed[1]], axis=1)
+    block_col = 4 * (iota((32, 128), 1) % 64) + 256 * t - 4
     code = ((flat // 8192 - (s - 2)) * 9 + flat % 8192 // 8 - block_col) * 8 + flat % 8
-    code = code.astype(F32).T.astype(jnp.int32)
     pick = iota((64, 128), 0)
     into = iota((64, 128), 1)
     counts = live[...].astype(F32)
@@ -398,15 +409,67 @@
         ref[...] = jnp.zeros_like(ref)
     turn(0)
 
-    for c in range(4):
-        relay(c)
+    row = iota((8, 128), 0) // 4
+    offset = jnp.where(lane < 64, 0.0, 4.0)
+    first_strip = jnp.where(s == 0, 1.0, 0.0)
+    last_strip = jnp.where(s == STRIPS - 1, 1.0, 0.0)
+
+    def row_share(a, k):
+        r = (2 * k + row).astype(F32)
+        if a == -1:
+            return hat(r + 4.0) * (1.0 - first_strip)
+        if a == 0:
+            return hat(r) + hat(r + 4.0) * first_strip
+        if a == 1:
+            return hat(r - 4.0) + hat(r - 8.0) * last_strip
+        return hat(r - 8.0) * (1.0 - last_strip)
+
+    left = iota((8, 8, 128), 2) < 64
+
+    def parted(x, share):
+        x = x * share[None]
+        high = x.astype(BF16).astype(F32)
+        return jnp.where(left, high, x - high)
+
+    def part(n, carry):
+        for k, a, ref in ((0, -1, top), (3, 1, low)):
+            x = turned[pl.ds(8 * n + 10, 8), k]
+            both = jnp.concatenate(
+                [parted(x, row_share(a, k)), parted(x, row_share(a + 1, k))], axis=2
+            )
+            ref[pl.ds(pl.multiple_of(64 * n + 80, 16), 64)] = both.reshape(64, 256).astype(BF16)
+        pieces = []
+        for k in (1, 2):
+            x = turned[pl.ds(8 * n + 10, 8), k]
+            pieces.append(
+                jnp.concatenate([parted(x, row_share(0, k)), parted(x, row_share(1, k))], axis=2)
+            )
+        both = jnp.stack(pieces, axis=1)
+        mid[pl.ds(pl.multiple_of(128 * n + 160, 16), 128)] = both.reshape(128, 256).astype(BF16)
+        return carry
+
+    relay(0)
+    relay(1)
     for copy in edges:
         copy.wait()
-    for j, slot in ((2, 2 + way), (0, 2 - way), (1, 2 - 2 * way), (3, 2 + 2 * way)):
-        if j:
-            for c in range(4):
-                for k in range(TASKS):
-                    windows[j, c, k].wait_recv()
+    for c in range(4):
+        for k in range(TASKS):
+            windows[2, c, k].wait_recv()
+    place(2 + way)
+    for copy in own_deeps:
+        copy.wait()
+    for copy in deeps:
+        copy.wait_recv()
+    for lev in (1, 2, 3):
+        turn(lev)
+    relay(2)
+    lax.fori_loop(0, 32, part, 0)
+    relay(3)
+    place(2 - way)
+    for j, slot in ((1, 2 - 2 * way), (3, 2 + 2 * way)):
+        for c in range(4):
+            for k in range(TASKS):
+                windows[j, c, k].wait_recv()
         place(slot)
 
     spot = iota((384, 128), 0)
@@ -571,45 +634,6 @@
 
         return carry
 
-    row = iota((8, 128), 0) // 4
-    offset = jnp.where(lane < 64, 0.0, 4.0)
-    first_strip = jnp.where(s == 0, 1.0, 0.0)
-    last_strip = jnp.where(s == STRIPS - 1, 1.0, 0.0)
-
-    def row_share(a, k):
-        r = (2 * k + row).astype(F32)
-        if a == -1:
-            return hat(r + 4.0) * (1.0 - first_strip)
-        if a == 0:
-            return hat(r) + hat(r + 4.0) * first_strip
-        if a == 1:
-            return hat(r - 4.0) + hat(r - 8.0) * last_strip
-        return hat(r - 8.0) * (1.0 - last_strip)
-
-    left = iota((8, 8, 128), 2) < 64
-
-    def parted(x, share):
-        x = x * share[None]
-        high = x.astype(BF16).astype(F32)
-        return jnp.where(left, high, x - high)
-
-    def part(n, carry):
-        for k, a, ref in ((0, -1, top), (3, 1, low)):
-            x = turned[pl.ds(8 * n + 10, 8), k]
-            both = jnp.concatenate(
-                [parted(x, row_share(a, k)), parted(x, row_share(a + 1, k))], axis=2
-            )
-            ref[pl.ds(pl.multiple_of(64 * n + 80, 16), 64)] = both.reshape(64, 256).astype(BF16)
-        pieces = []
-        for k in (1, 2):
-            x = turned[pl.ds(8 * n + 10, 8), k]
-            pieces.append(
-                jnp.concatenate([parted(x, row_share(0, k)), parted(x, row_share(1, k))], axis=2)
-            )
-        both = jnp.stack(pieces, axis=1)
-        mid[pl.ds(pl.multiple_of(128 * n + 160, 16), 128)] = both.reshape(128, 256).astype(BF16)
-        return carry
-
     def col_share(g):
         first = jnp.where((g == 0) & (t == 0), 1.0, 0.0)
         last = jnp.where((g == 31) & (t == TASKS - 1), 1.0, 0.0)
@@ -678,13 +702,6 @@
 
     lax.fori_loop(0, SOLVES - 1, solve, 0)
 
-    own_deep.wait()
-    for copy in deeps:
-        copy.wait_recv()
-    for lev in (1, 2, 3):
-        turn(lev)
-    lax.fori_loop(0, 32, part, 0)
-
     def arrived(i, carry):
         for copy in rows_of(i):
             copy.wait_recv()
@@ -729,6 +746,7 @@
             pltpu.VMEM((16, 4, 8, 1024), F32),
             pltpu.VMEM((8, 1024), jnp.int32),
             pltpu.VMEM((4, 2, 2, 8, 1024), F32),
+            pltpu.VMEM((4, 8, 32, 128), F32),
             pltpu.VMEM((16, 8, 1024), F32),
             pltpu.VMEM((16, 3, 8, 1024), F32),
             pltpu.VMEM((4, 8, 128), F32),
@@ -754,9 +772,9 @@
             pltpu.VMEM((SPAN, 4, 8, 128), F32),
             pltpu.VMEM((64, 4, 8, 256), F32),
             dma((8,)), dma((8,)), dma((2,)), dma((2,)), dma((4,)), dma((4,)),
-            dma((9,)), dma((12,)), dma((12,)), dma((3,)), dma((3,)),
+            dma((13,)), dma((12,)), dma((12,)), dma((3,)), dma((3,)),
             dma((64,)), dma((64,)), dma((4,)), dma((4,)),
-            dma((3,)), dma((3,)), dma((2, SOLVES)), dma((2, SOLVES)),
+            dma((12,)), dma((12,)), dma((2, SOLVES)), dma((2, SOLVES)),
             dma((4,)), dma((4,)), dma((4,)), dma((4,)), dma((6,)), dma((6,)),
         ],
         compiler_params=pltpu.CompilerParams(
@@ -786,7 +804,7 @@
         obs_pos.reshape(64, 128),
         obs_value.reshape(64, 128),
         obs_var.reshape(64, 128),
-        observation_list.reshape(128, 32),
+        observation_list.transpose(0, 2, 1),
         obs_count,
     )
 

time: 116 us -> 119 us (1.026)
  Pallas kernels: 111 us -> 115 us
  local copies, waits for them, and re-layouts: 4.63 us -> 3.16 us
    pallas_call x1, Pallas kernels: 111 us -> 115 us  [assimilate(): pl.pallas_call(kernel, out_shape=jax.ShapeDtypeStruct((16, 4, 8, 1024), F...]
    unnamed x2 -> x1, local copies, waits for them, and re-layouts: 4.63 us -> 3.16 us
where the time goes in v4:
time: 119 us
  Pallas kernels  115 us (97%)
  local copies, waits for them, and re-layouts  3.16 us (3%)
    pallas_call x1, Pallas kernels, assimilate(): pl.pallas_call(kernel, out_shape=jax.ShapeDtypeStruct((16, 4, 8, 1024), F...  115 us
    unnamed x1, local copies, waits for them, and re-layouts  3.16 us

profile of v4, /device:TPU:0, one launch (start us, length us, event | category | flops | bytes accessed | tf_op | source)
XLA Modules:
  0.0 118.6 jit_solution(1030471360600099642)
XLA Ops:
  0.0 115.4 %shard_map.100 = f32[16,4,8,1024]{3,2,1,0:T(8,128)} custom-call(f32[16,4,8,1024]{3,2,1,0:T(8,128)} %x.1, s32[8,1024]{1,0:T(8,128)} %wet.1, s32[4,8,1024]{2,1,0:T(8,128)} %donor.1, f32[4,8,1024]{2,1,0:T(8,128)} %frac.1, f32[4]{0:T(128)} %rate.1, s32[64,128]{1,0:T(8,128)} %bitcast.4, f32[64,128]{1,0:T(8,128)} %bitcast.5, f32[64,128]{1,0:T(8,128)} %bitcast.6, ...), custom_call_target="tpu_custom_call" | custom-call | tf_op jit(solution)/shard_map/pallas_call | solution.py:740
  115.4 3.2 %copy.12 = f32[16,4,8,1024]{3,2,1,0:T(8,128)} copy(f32[16,4,8,1024]{3,2,1,0:T(8,128)} %shard_map.100) | data formatting | bytes 4194304

commit v5 on v4

--- a/solution.py
+++ b/solution.py
@@ -252,6 +252,9 @@
             swaps[c, k] = send(
                 fs0.at[chunk, :, cols], w5.at[2, block(t, c)], swap_s.at[i], swap_r.at[i], (to, s)
             )
+
+    def deepen(c):
+        chunk = pl.ds(4 * c, 4)
         copy = pltpu.make_async_copy(
             fs1.at[chunk, :, :, here_cols], f1.at[block(t, c)], own.at[9 + c]
         )
@@ -314,6 +317,8 @@
         if c:
             forward(c - 1)
     forward(3)
+    for c in range(4):
+        deepen(c)
     own_rim.wait()
     for copy in rims:
         copy.wait_recv()
@@ -448,23 +453,14 @@
         mid[pl.ds(pl.multiple_of(128 * n + 160, 16), 128)] = both.reshape(128, 256).astype(BF16)
         return carry
 
-    relay(0)
-    relay(1)
     for copy in edges:
         copy.wait()
     for c in range(4):
         for k in range(TASKS):
             windows[2, c, k].wait_recv()
     place(2 + way)
-    for copy in own_deeps:
-        copy.wait()
-    for copy in deeps:
-        copy.wait_recv()
-    for lev in (1, 2, 3):
-        turn(lev)
-    relay(2)
-    lax.fori_loop(0, 32, part, 0)
-    relay(3)
+    for c in range(4):
+        relay(c)
     place(2 - way)
     for j, slot in ((1, 2 - 2 * way), (3, 2 + 2 * way)):
         for c in range(4):
@@ -701,6 +697,14 @@
         return copies
 
     lax.fori_loop(0, SOLVES - 1, solve, 0)
+
+    for copy in own_deeps:
+        copy.wait()
+    for copy in deeps:
+        copy.wait_recv()
+    for lev in (1, 2, 3):
+        turn(lev)
+    lax.fori_loop(0, 32, part, 0)
 
     def arrived(i, carry):
         for copy in rows_of(i):

time: 119 us -> 110 us (0.924)
  Pallas kernels: 115 us -> 107 us
    pallas_call x1, Pallas kernels: 115 us -> 107 us  [assimilate(): pl.pallas_call(kernel, out_shape=jax.ShapeDtypeStruct((16, 4, 8, 1024), F...]
where the time goes in v5:
time: 110 us
  Pallas kernels  107 us (97%)
  local copies, waits for them, and re-layouts  3.16 us (3%)
    pallas_call x1, Pallas kernels, assimilate(): pl.pallas_call(kernel, out_shape=jax.ShapeDtypeStruct((16, 4, 8, 1024), F...  107 us
    unnamed x1, local copies, waits for them, and re-layouts  3.16 us

profile of v5, /device:TPU:0, one launch (start us, length us, event | category | flops | bytes accessed | tf_op | source)
XLA Modules:
  0.0 110.2 jit_solution(18207606574775935042)
XLA Ops:
  0.0 107.1 %shard_map.100 = f32[16,4,8,1024]{3,2,1,0:T(8,128)} custom-call(f32[16,4,8,1024]{3,2,1,0:T(8,128)} %x.1, s32[8,1024]{1,0:T(8,128)} %wet.1, s32[4,8,1024]{2,1,0:T(8,128)} %donor.1, f32[4,8,1024]{2,1,0:T(8,128)} %frac.1, f32[4]{0:T(128)} %rate.1, s32[64,128]{1,0:T(8,128)} %bitcast.4, f32[64,128]{1,0:T(8,128)} %bitcast.5, f32[64,128]{1,0:T(8,128)} %bitcast.6, ...), custom_call_target="tpu_custom_call" | custom-call | tf_op jit(solution)/shard_map/pallas_call | solution.py:744
  107.1 3.2 %copy.12 = f32[16,4,8,1024]{3,2,1,0:T(8,128)} copy(f32[16,4,8,1024]{3,2,1,0:T(8,128)} %shard_map.100) | data formatting | bytes 4194304
